TPU v7x, 32 devices: a whole 2x2x4 slice. The times are simulated.
32 devices in a mesh: wide: 8 (over z, y), narrow: 4 (over x, core).
Axes of the slice: x: 2, y: 2, z: 4, core: 2. Of those that a mesh axis runs over, the one named last changes fastest.
Arguments:
- images: bfloat16 [704, 16, 16, 256], P(('wide', 'narrow')), may hold values from -6 to 6
- time_embed: bfloat16 [704, 512], P(('wide', 'narrow')), may hold values from -6 to 6
- out_cotangent: bfloat16 [704, 16, 16, 256], P(('wide', 'narrow')), may hold values from -6 to 6
- conv_master: float32 [2, 9, 256, 256], P(None, None, ('wide', 'narrow')), may hold values from -0.125 to 0.125
- dense_master: float32 [512, 256], P(('wide', 'narrow')), may hold values from -0.25 to 0.25
- attn_master: float32 [4, 256, 256], P(None, ('wide', 'narrow'))
- vector_master: float32 [12, 256], P(None, ('wide', 'narrow'))
- vector_first: float32 [12, 256], P(None, ('wide', 'narrow'))
- vector_second: float32 [12, 256], P(None, ('wide', 'narrow')), as said below
- owners: int32 [23], replicated, may hold values from 0 to 31, as said below
- slot_first: float32 [32, 512, 256], P(('wide', 'narrow'))
- slot_second: float32 [32, 512, 256], P(('wide', 'narrow')), as said below
- slot_left_basis: float32 [32, 512, 512], P(('wide', 'narrow')), as said below
- slot_right_basis: float32 [32, 256, 256], P(('wide', 'narrow')), as said below
- slot_left_stat: float32 [32, 512, 512], P(('wide', 'narrow')), as said below
- slot_right_stat: float32 [32, 256, 256], P(('wide', 'narrow')), as said below
Outputs:
- activations: bfloat16 [704, 16, 16, 256], P(('wide', 'narrow'))
- image_grad: float32 [704, 16, 16, 256], P(('wide', 'narrow'))
- time_grad: float32 [704, 512], P(('wide', 'narrow'))
- conv_new: float32 [2, 9, 256, 256], P(None, None, ('wide', 'narrow'))
- dense_new: float32 [512, 256], P(('wide', 'narrow'))
- attn_new: float32 [4, 256, 256], P(None, ('wide', 'narrow'))
- vector_new: float32 [12, 256], P(None, ('wide', 'narrow'))
- conv_copy: bfloat16 [2, 9, 256, 256], P(None, None, ('wide', 'narrow'))
- dense_copy: bfloat16 [512, 256], P(('wide', 'narrow'))
- attn_copy: bfloat16 [4, 256, 256], P(None, ('wide', 'narrow'))
- vector_copy: bfloat16 [12, 256], P(None, ('wide', 'narrow'))
- vector_first_new: float32 [12, 256], P(None, ('wide', 'narrow'))
- vector_second_new: float32 [12, 256], P(None, ('wide', 'narrow'))
- slot_first_new: float32 [32, 512, 256], P(('wide', 'narrow'))
- slot_second_new: float32 [32, 512, 256], P(('wide', 'narrow'))
- left_basis_new: float32 [32, 512, 512], P(('wide', 'narrow'))
- right_basis_new: float32 [32, 256, 256], P(('wide', 'narrow'))
- left_stat_new: float32 [32, 512, 512], P(('wide', 'narrow'))
- right_stat_new: float32 [32, 256, 256], P(('wide', 'narrow'))
Inputs may be any that keep to these rules, and one draw needn't show every extreme that they name: `owners`: Twenty-three different device numbers, counted over wide and narrow together with wide the slower. `slot_left_basis`: in each slot the leading block is orthogonal, of order 512 in the slot of the time projection's owner and 256 elsewhere; the rest is zero. `slot_right_basis`: each slot is orthogonal. `slot_left_stat`: in each slot the leading block (of the same order as the basis) is symmetric with a positive, strictly dominant diagonal; the rest is zero. `slot_right_stat`: each slot is symmetric with a positive, strictly dominant diagonal. `slot_second`: every entry is positive. `vector_second`: every entry is positive.
All inputs are finite; a program needn't handle non-finite values.
Results may differ from a plain program's by a relative error of at most 0.018.
The roundings to bfloat16 on the way count: a program that leaves them out, or rounds other values in their place, can miss the bound.
Values may be sent and summed in bfloat16 or wider, within the bound.
A program may use at most 576 MiB of HBM per device.

v0:
```python
import functools

import jax
import jax.numpy as jnp
from jax import lax
from jax.experimental import pallas as pl
from jax.experimental.pallas import tpu as pltpu
from jax.sharding import PartitionSpec as P

BF = jnp.bfloat16
F32 = jnp.float32
STEP = 10
GROUP = 8
BLK = 128
half_root = 0.5**0.5
norm_eps = 1e-6
adam_eps = 1e-8
HI = lax.Precision.HIGHEST
MESH = pl.DeviceIdType.MESH
AXES = ("wide", "narrow")
MATS = 22
VMEM = pl.BlockSpec(memory_space=pltpu.VMEM)
SMEM = pl.BlockSpec(memory_space=pltpu.SMEM)
ANY = pl.BlockSpec(memory_space=pl.ANY)
LIMIT = 56 << 20
TOGETHER = 6

def mm(a,b):
    return lax.dot_general(a,b,(((1,),(0,)),((),())),preferred_element_type=F32)
def mm_nt(a,b):
    return lax.dot_general(a,b,(((1,),(1,)),((),())),preferred_element_type=F32)
def mm_tn(a,b):
    return lax.dot_general(a,b,(((0,),(0,)),((),())),preferred_element_type=F32)

def group_sum(v):
    lane=lax.broadcasted_iota(jnp.int32, v.shape, 1)
    n=v.shape[1]
    for s in (1,2,4):
        v=v+jnp.where((lane & s)==0, pltpu.roll(v,n-s,1), pltpu.roll(v,s,1))
    return v

def col_sum(v):
    return jnp.sum(v,axis=0,keepdims=True)

def pad8(v):
    return jnp.broadcast_to(v,(8,v.shape[1]))

def group_mean(colsum, count):
    return group_sum(pad8(colsum))[0:1]*(1.0/count)

def normal_form(v):
    count=v.shape[0]*GROUP
    m=group_mean(col_sum(v),count)
    yield
    c=v-m
    var=group_mean(col_sum(c*c),count)
    yield
    r=lax.rsqrt(var+norm_eps)
    return c*r, r

def norm_back(grad, xhat, r, gain):
    count=grad.shape[0]*GROUP
    shift_grad=col_sum(grad)
    gain_grad=col_sum(grad*xhat)
    m1=group_mean(shift_grad*gain,count)
    m2=group_mean(gain_grad*gain,count)
    yield
    return (grad*(gain*r)-(m1*r)-xhat*(m2*r)), gain_grad, shift_grad

def sigmoid(y):
    return pl.reciprocal(1.0+jnp.exp(-y),approx=True)

def spread(ref, i, v, side):
    tokens, c = v.shape
    x=lax.broadcasted_iota(jnp.int32,(tokens,1),0) & (side-1)
    before=jnp.where(x==0,0.0,pltpu.roll(v,1,0)).astype(BF)
    after=jnp.where(x==side-1,0.0,pltpu.roll(v,tokens-1,0)).astype(BF)
    ref[i,side:side+tokens,0:c]=before
    ref[i,side:side+tokens,c:2*c]=v.astype(BF)
    ref[i,side:side+tokens,2*c:3*c]=after

def taps(ref, count, dy, tokens, side):
    return jnp.concatenate([ref[i,side*dy:side*dy+tokens,:] for i in range(count)],axis=0)

def train_body(side, owners_ref, img_ref, cot_ref, emb_ref, w_ref,
         act_ref, igrad_ref, tgrad_ref, gw_ref, gvec_ref, inv_ref,
         dense_ref, vec_ref, wt, acc, gvec, proj, pgrad, p1, p2, s2, s1):
    step=pl.program_id(0); steps=pl.num_programs(0)
    ib,tokens,c=img_ref.shape
    batch=emb_ref.shape[0]
    scale=c**-0.5

    @pl.when(step==0)
    def _():
        acc[...]=jnp.zeros_like(acc)
        gvec[...]=jnp.zeros_like(gvec)
        pgrad[...]=jnp.zeros_like(pgrad)
        for ref in (p1,p2,s2,s1):
            for i in range(ib):
                z=jnp.zeros((side,3*c),BF)
                ref[i,0:side,:]=z
                ref[i,side+tokens:2*side+tokens,:]=z
        for k in range(2):
            for t in range(9):
                wt[k, 8-t]=w_ref[9*k+t].T
        chips=c//16
        total=jnp.zeros((16,c),F32)
        for o in range(chips):
            total=total+w_ref[24,16*o:16*o+16].astype(F32)
            for h in range(2):
                dense_ref[32*o+16*h:32*o+16*h+16]=w_ref[22+h,16*o:16*o+16]
        vec_ref[...]=total
        for d in range(inv_ref.shape[0]):
            inv_ref[d]=-1
        for m in range(owners_ref.shape[0]):
            inv_ref[owners_ref[m]]=m if m<9 else MATS if m==9 else m-1
        e=emb_ref[...].astype(F32)
        proj[0:batch]=mm((e*sigmoid(e)).astype(BF),dense_ref[...])+total[7:8]

    vec=vec_ref[...]
    row=lambda k: vec[k:k+1]

    up=lambda t: t.astype(F32)
    sums={}
    def add(kk,val):
        sums[kk]=val if kk not in sums else sums[kk]+val
    def three(ref,k,dy):
        return jnp.concatenate([ref[k+3*dy+dx] for dx in range(3)],axis=0)
    def conv(ref,i,weight):
        out=None
        for dy in range(3):
            part=mm(ref[i,side*dy:side*dy+tokens,:],weight(dy))
            out=part if out is None else out+part
            yield
        return out
    def wgrad(base,aref,gref,i):
        at=aref[i,side:side+tokens,c:2*c].T
        for dy in range(3):
            g=mm(at,gref[i,side*dy:side*dy+tokens,:])
            for dx in range(3):
                acc[base+8-(3*dy+dx)]+=g[:,dx*c:(dx+1)*c]
            yield
    def swish_back(grad,h,gain,shift):
        y=h*gain+shift
        s=sigmoid(y)
        return grad*(s*(1.0+y*(1.0-s)))

    def image(i):
        x=img_ref[i].astype(F32)
        h0,r0=yield from normal_form(x)
        y=h0*row(0)+row(3)
        spread(p1,i,y*sigmoid(y),side)
        yield
        t=yield from conv(p1,i,lambda dy: three(w_ref,0,dy))
        t=t+(row(6)+proj[pl.ds(step*ib+i,1),:])
        h1,r1=yield from normal_form(t)
        y=h1*row(1)+row(4)
        spread(p2,i,y*sigmoid(y),side)
        yield
        t=yield from conv(p2,i,lambda dy: three(w_ref,9,dy))
        mid=(x+(t+row(8)))*half_root
        h2,r2=yield from normal_form(mid)
        normed=(h2*row(2)+row(5)).astype(BF)
        yield
        q=(mm(normed,w_ref[18])+row(9)).astype(BF)
        k=mm(normed,w_ref[19]).astype(BF)
        yield
        v=(mm(normed,w_ref[20])+row(10)).astype(BF)
        sc=mm_nt(q,k)*scale
        yield
        e=jnp.exp(sc-jnp.max(sc,axis=1,keepdims=True))
        a=e/jnp.sum(e,axis=1,keepdims=True)
        low=a.astype(BF)
        yield
        mixed=mm(low,v).astype(BF)
        cot=cot_ref[i].astype(F32)*half_root
        bg=cot.astype(BF)
        mg=mm_nt(bg,w_ref[21]).astype(BF)
        add(11,col_sum(up(bg)))
        yield
        branch=mm(mixed,w_ref[21])+row(11)
        pg=mm_nt(mg,v)
        act_ref[i]=((mid+branch)*half_root).astype(BF)
        yield
        sg=(a*(pg-jnp.sum(a*pg,axis=1,keepdims=True))).astype(BF)
        acc[21]+=mm_tn(mixed,bg)
        vg=mm_tn(low,mg).astype(BF)
        yield
        qg=(mm(sg,k)*scale).astype(BF)
        kg=(mm_tn(sg,q)*scale).astype(BF)
        yield
        ng=mm_nt(qg,w_ref[18])+mm_nt(kg,w_ref[19])+mm_nt(vg,w_ref[20])
        yield
        normed_t=normed.T
        acc[18]+=mm(normed_t,qg)
        acc[19]+=mm(normed_t,kg)
        acc[20]+=mm(normed_t,vg)
        add(9,col_sum(up(qg)));add(10,col_sum(up(vg)))
        yield
        d,gg,gs=yield from norm_back(ng,h2,r2,row(2))
        add(2,gg);add(5,gs)
        midg=cot+d
        g=up((midg*half_root).astype(BF))
        add(8,col_sum(g))
        spread(s2,i,g,side)
        yield
        ag=yield from conv(s2,i,lambda dy: three(wt.at[1],0,dy))
        d=swish_back(ag,h1,row(1),row(4))
        yield
        yield from wgrad(9,p2,s2,i)
        d,gg,gs=yield from norm_back(d,h1,r1,row(1))
        add(1,gg);add(4,gs)
        g=up(d.astype(BF))
        s=col_sum(g)
        add(6,s)
        pgr=up(s.astype(BF))
        pgrad[pl.ds(step*ib+i,1),:]=pgr
        add(7,pgr)
        spread(s1,i,g,side)
        yield
        ag=yield from conv(s1,i,lambda dy: three(wt.at[0],0,dy))
        d=swish_back(ag,h0,row(0),row(3))
        yield
        yield from wgrad(0,p1,s1,i)
        d,gg,gs=yield from norm_back(d,h0,r0,row(0))
        add(0,gg);add(3,gs)
        igrad_ref[i]=midg*half_root+d

    def run(count):
        sums.clear()
        live=[image(i) for i in range(count)]
        while live:
            for g in list(live):
                try: next(g)
                except StopIteration: live.remove(g)
        gvec[0:12]+=jnp.concatenate([sums[j] for j in range(12)],axis=0)
    rest=batch-ib*(-(-batch//ib)-1)
    if rest==ib: run(ib)
    else:
        @pl.when(step<steps-1)
        def _(): run(ib)
        @pl.when(step==steps-1)
        def _(): run(rest)

    @pl.when(step==steps-1)
    def _():
        for m in range(acc.shape[0]):
            gw_ref[m]=acc[m].astype(BF)
        gvec_ref[...]=gvec[...]
        e=emb_ref[...].astype(F32)
        s=sigmoid(e)
        ea=(e*s).astype(BF)
        pg=pgrad[0:batch].astype(BF)
        tgrad_ref[...]=mm_nt(pg,dense_ref[...])*(s*(1.0+e*(1.0-s)))
        gd=mm_tn(ea,pg).astype(BF)
        for o in range(c//16):
            for h in range(2):
                gw_ref[22+h,16*o:16*o+16]=gd[32*o+16*h:32*o+16*h+16]

def train_images(owners,images,cot,embed,w,side,ndev):
    batch,tokens,c=images.shape
    emb=embed.shape[1]
    ib=min(TOGETHER,batch)
    rows=-(-batch//8)*8
    whole=lambda a: pl.BlockSpec(a.shape,lambda s: (0,)*len(a.shape))
    blk=pl.BlockSpec((ib,tokens,c),lambda s:(s,0,0))
    sd=jax.ShapeDtypeStruct
    outs=[sd((batch,tokens,c),BF),sd((batch,tokens,c),F32),sd((batch,emb),F32),sd((MATS+2,c,c),BF),sd((16,c),F32)]
    return pl.pallas_call(functools.partial(train_body,side),grid=(-(-batch//ib),),
        in_specs=[SMEM,blk,blk,whole(embed),whole(w)],
        out_specs=[blk,blk]+[whole(o) for o in outs[2:]]+[SMEM],
        out_shape=outs+[sd((ndev,),jnp.int32)],
        scratch_shapes=[pltpu.VMEM((emb,c),BF),pltpu.VMEM((16,c),F32),pltpu.VMEM((2,9,c,c),BF),pltpu.VMEM((MATS,c,c),F32),pltpu.VMEM((16,c),F32),pltpu.VMEM((rows,c),F32),pltpu.VMEM((rows,c),F32)]
          +[pltpu.VMEM((ib,tokens+2*side,3*c),BF)]*4,
        compiler_params=pltpu.CompilerParams(vmem_limit_bytes=LIMIT),
        name="train_images")(owners,images,cot,embed,w)

def fdot(a,b,ca,cb):
    return lax.dot_general(a,b,(((ca,),(cb,)),((),())),precision=HI,preferred_element_type=F32)
nn=lambda a,b: fdot(a,b,1,0)
nt=lambda a,b: fdot(a,b,1,1)
tn=lambda a,b: fdot(a,b,0,0)

def inverse_factors(blocks):
    n=BLK
    lane=lax.broadcasted_iota(jnp.int32,(8,n),1)
    sub=lax.broadcasted_iota(jnp.int32,(8,n),0)
    tables=[[b[8*v:8*v+8] for v in range(n//8)] for b in blocks]
    over_lanes=lambda t,j: jnp.broadcast_to(t[:,j:j+1],(8,n))
    over_rows=lambda t,i: jnp.broadcast_to(t[i:i+1],(8,n))
    for J in range(n//8):
        lo=8*J
        in_block=(lane>=lo)&(lane<lo+8)
        for t in tables:
            cur=t[J]
            cols=[over_lanes(cur,lo+j) for j in range(8)]
            m=[[over_rows(cols[j],i) for j in range(i+1)] for i in range(8)]
            R=[jnp.where(in_block,jnp.where(lane==lo+i,1.0,0.0),over_rows(cur,i)) for i in range(8)]
            r=[None]*8
            l=[[None]*8 for _ in range(8)]
            for k in range(8):
                d=m[k][k]
                r[k]=pl.reciprocal(d,approx=True)
                for i in range(k+1,8):
                    l[i][k]=m[i][k]*r[k]
                for i in range(k+1,8):
                    for j in range(k+1,i+1):
                        m[i][j]=m[i][j]-l[i][k]*m[j][k]
                    R[i]=R[i]-l[i][k]*R[k]
            P=[None]*8
            for k in range(7,-1,-1):
                P[k]=R[k]*r[k]
                for i in range(7,k,-1):
                    P[k]=P[k]-l[i][k]*P[i]
            done=R[0]*lax.rsqrt(m[0][0])
            for i in range(1,8):
                done=jnp.where(sub==i,R[i]*lax.rsqrt(m[i][i]),done)
            t[J]=jnp.where(lane<=lo+sub,done,0.0)
            for v in range(J+1,n//8):
                new=jnp.where(in_block,0.0,t[v])
                for k in range(8):
                    new=new-over_lanes(t[v],lo+k)*P[k]
                t[v]=new
    return [jnp.concatenate(t,axis=0) for t in tables]

def at(k,size):
    return pl.ds(pl.multiple_of(k*size,size),size)

def split(x):
    hi=x.astype(BF)
    return hi,(x-hi.astype(F32)).astype(BF)

def bdot(a,b,ca,cb):
    return lax.dot_general(a,b,(((ca,),(cb,)),((),())),preferred_element_type=F32)

def dot3(a,b,ca,cb):
    (ah,al),(bh,bl)=split(a),split(b)
    return bdot(ah,bh,ca,cb)+(bdot(ah,bl,ca,cb)+bdot(al,bh,ca,cb))

def dot2(a,b,ca,cb):
    ah,al=split(a)
    return bdot(ah,b,ca,cb)+bdot(al,b,ca,cb)

def factor_both(a_l, g_l, a_r, g_r):
    for p in range(g_l.shape[0]//BLK):
        lo,hi=p*BLK,(p+1)*BLK
        live=[(a,g) for a,g in ((a_l,g_l),(a_r,g_r)) if g.shape[0]>lo]
        invs=inverse_factors([g[lo:hi,lo:hi] for _,g in live])
        for (a,g),inv in zip(live,invs):
            q=dot3(a[:,lo:hi],inv,1,1)
            if hi<g.shape[0]:
                r=nn(inv,g[lo:hi,hi:])
                g[hi:,hi:]=g[hi:,hi:]-tn(r,r)
                a[:,hi:]=a[:,hi:]-dot3(q,r,1,0)
            a[:,lo:hi]=q

def soap(nb, grad, ins, outs, update, g_l, g_r):
    (first,second,left,right,lstat,rstat)=ins
    first_o,second_o,left_o,right_o,lstat_o,rstat_o=outs
    c=right.shape[0]
    big=left.shape[0]
    g=grad[...]
    L=left[...]; Rb=right[...]
    ls=0.95*lstat[...]+0.05*bdot(g,g,1,1)
    rs=0.95*rstat[...]+0.05*bdot(g,g,0,0)
    lstat_o[...]=ls; rstat_o[...]=rs
    ar=nn(rs,Rb)
    right_o[...]=ar
    g_r[...]=tn(ar,ar)
    al=nn(ls,L)
    left_o[...]=al
    unit=(lax.broadcasted_iota(jnp.int32,(big,big),0)==lax.broadcasted_iota(jnp.int32,(big,big),1))&(lax.broadcasted_iota(jnp.int32,(big,big),0)>=nb*c)
    g_l[...]=tn(al,al)+jnp.where(unit,1.0,0.0)
    corr=1.0-0.5**STEP
    turned=dot3(dot2(L,g,0,0),Rb,1,0)
    inside=lax.broadcasted_iota(jnp.int32,(big,c),0)<nb*c
    moment=jnp.where(inside,0.5*first[...]+0.5*turned,0.0)
    sec=jnp.where(inside,0.5*second[...]+0.5*turned*turned,0.0)
    first_o[...]=moment; second_o[...]=sec
    direction=moment/corr/(jnp.sqrt(sec/corr)+adam_eps)
    update[...]=dot3(dot3(L,direction,1,0),Rb,1,1)
    factor_both(left_o,g_l,right_o,g_r)

def owner_body(inv_ref, q_ref, *refs):
    ins_hbm=refs[0:6]; outs_hbm=refs[6:12]; send_o=refs[12]
    ins=refs[13:19]; outs=refs[19:25]
    grad,update,g_l,g_r,in_sem,out_sem=refs[25:]
    me=lax.axis_index("wide")*lax.axis_size("narrow")+lax.axis_index("narrow")
    held=inv_ref[me]
    kind=jnp.where(held<0,0,jnp.where(held==MATS,2,1))
    c=ins[3].shape[1]; big=ins[2].shape[1]
    copies_in=[pltpu.make_async_copy(h.at[0],v,in_sem.at[i]) for i,(h,v) in enumerate(zip(ins_hbm,ins))]
    copies_out=[pltpu.make_async_copy(v,h.at[0],out_sem.at[i]) for i,(h,v) in enumerate(zip(outs_hbm,outs))]
    for cp in copies_in: cp.start()
    @pl.when(kind==1)
    def _():
        grad[...]=jnp.zeros_like(grad)
        for i in range(big//32):
            grad[16*i:16*i+16]=q_ref[32*i:32*i+16]
    @pl.when(kind==2)
    def _():
        grad[...]=q_ref[...]
    for cp in copies_in: cp.wait()
    ndev=send_o.shape[0]
    @pl.when(kind==0)
    def _():
        for o in outs: o[...]=jnp.zeros_like(o)
        send_o[...]=jnp.zeros_like(send_o)
    @pl.when(kind>0)
    def _():
        soap(kind,grad,ins,outs,update,g_l,g_r)
    for size,number in ((c,1),(big,2)):
        @pl.when(kind==number)
        def _():
            r=size//ndev
            for d in range(ndev):
                u=update[r*d:r*d+r]
                if r<16: u=jnp.concatenate([u,jnp.zeros((16-r,c),F32)],axis=0)
                send_o[d]=u.astype(BF)
    for cp in copies_out: cp.start()
    for cp in copies_out: cp.wait()

def owner_step(inv,q,first,second,left,right,lstat,rstat,ndev):
    c=right.shape[1]; big=left.shape[1]
    slots=(first,second,left,right,lstat,rstat)
    sd=lambda a: jax.ShapeDtypeStruct(a.shape,F32)
    vm=pl.BlockSpec(memory_space=pltpu.VMEM); hb=pl.BlockSpec(memory_space=pl.ANY)
    buf=lambda a: pltpu.VMEM(a.shape[1:],F32)
    return pl.pallas_call(owner_body,
        in_specs=[pl.BlockSpec(memory_space=pltpu.SMEM),vm]+[hb]*6,
        out_specs=[hb]*6+[vm],
        out_shape=[sd(a) for a in slots]+[jax.ShapeDtypeStruct((ndev,16,c),BF)],
        scratch_shapes=[buf(a) for a in slots]*2+[pltpu.VMEM((big,c),BF),pltpu.VMEM((big,c),F32)]+[pltpu.VMEM((big,big),F32),pltpu.VMEM((c,c),F32),
          pltpu.SemaphoreType.DMA((6,)),pltpu.SemaphoreType.DMA((6,))],
        compiler_params=pltpu.CompilerParams(vmem_limit_bytes=LIMIT),
        name="owner_step")(inv,q,*slots)

def place():
    w,n=lax.axis_index("wide"),lax.axis_index("narrow")
    return lax.div(w,2),lax.rem(w,2),lax.div(n,2),lax.rem(n,2)

def device(z,y,x,core):
    return (z*2+y,x*2+core)

def chip_of(z,y,x):
    return (z*2+y)*2+x

def greet(partners):
    barrier=pltpu.get_barrier_semaphore()
    count=0
    for dev,cond in partners:
        if cond is None:
            pl.semaphore_signal(barrier,inc=1,device_id=dev,device_id_type=MESH)
            count=count+1
        else:
            @pl.when(cond)
            def _():
                pl.semaphore_signal(barrier,inc=1,device_id=dev,device_id_type=MESH)
            count=count+jnp.where(cond,1,0)
    pl.semaphore_wait(barrier,count)

def remote(src,dst,send,recv,dev):
    return pltpu.make_async_remote_copy(src_ref=src,dst_ref=dst,send_sem=send,recv_sem=recv,device_id=dev,device_id_type=MESH)

GATHER=MATS+4
SHARE=GATHER//2
CUT=(SHARE+1)//2

def gather_body(depth, conv_ref, dense_ref, attn_ref, vec_ref, w_ref, part, vbuf,
                pair_s, pair_r, own_r, twin_r, up_s, down_s, x_s, y_s, twin_s):
    z,y,x,core=place()
    me=chip_of(z,y,x)
    rank=me*2+core
    twin=device(z,y,x,1-core)
    greet([(twin,None),(device(z,y,1-x,core),None),(device(z,1-y,x,core),None),
           (device(z-1,y,x,core),z>0),(device(z+1,y,x,core),z<depth-1)])
    conv=conv_ref.shape[0]
    part[0,0:conv]=conv_ref[...]
    part[0,conv:MATS]=attn_ref[...]
    part[0,MATS]=dense_ref[0:8]
    part[0,MATS+1]=dense_ref[8:16]
    cols,rows_v=vec_ref.shape
    vbuf[...]=jnp.zeros_like(vbuf)
    vbuf[0:cols,0:rows_v]=vec_ref[...]
    turned=vbuf[0:8,0:128].T[0:16]
    vbuf[...]=jnp.zeros_like(vbuf)
    vbuf[:,0:8]=turned
    mine=pltpu.roll(vbuf[...],rank*cols,1)
    part[0,MATS+2]=mine[0:8]
    part[0,MATS+3]=mine[8:16]
    swap=remote(part.at[0],part.at[1],pair_s,pair_r,twin)
    swap.start()
    rows=lambda o: pl.ds(pl.multiple_of(o*16,16),16)
    swap.wait()
    even,odd=core,1-core
    for m in range(MATS):
        w_ref[m,rows(me)]=jnp.concatenate([part[even,m],part[odd,m]],axis=0).astype(BF)
    for h,src in ((0,even),(1,odd)):
        w_ref[MATS+h,rows(me)]=jnp.concatenate([part[src,MATS],part[src,MATS+1]],axis=0).astype(BF)
    w_ref[MATS+2,rows(me)]=jnp.concatenate([part[0,MATS+2]+part[1,MATS+2],part[0,MATS+3]+part[1,MATS+3]],axis=0).astype(BF)
    w_ref[MATS+3,rows(me)]=jnp.zeros((16,w_ref.shape[2]),BF)

    def block(h,o,whose=core):
        return w_ref.at[pl.ds(SHARE*whose+(0,CUT)[h],(CUT,SHARE-CUT)[h]),rows(o)]
    def copy(h,o,send,recv,dev):
        return remote(block(h,o),block(h,o),send,recv.at[h,o],dev)
    def arrived(h,o):
        copy(h,o,pair_s,own_r,twin).wait_recv()
    side_x,side_y=device(z,y,1-x,core),device(z,1-y,x,core)
    to_x=lambda h,o: copy(h,o,x_s.at[h,o],own_r,side_x)
    to_y=lambda h,o: copy(h,o,y_s.at[h,o],own_r,side_y)
    to_twin=lambda h,o: copy(h,o,twin_s.at[h,o],twin_r,twin)
    to_up=lambda h,o: copy(h,o,up_s.at[h,o],own_r,device(z+1,y,x,core))
    to_down=lambda h,o: copy(h,o,down_s.at[h,o],own_r,device(z-1,y,x,core))

    def line(zz,wait,up,down):
        o=chip_of(zz,y,x)
        for h in range(2):
            if wait: arrived(h,o)
            if up:
                @pl.when(z<depth-1)
                def _(): to_up(h,o).start()
            if down:
                @pl.when(z>0)
                def _(): to_down(h,o).start()
            first,second=((to_x,to_y),(to_y,to_x))[h]
            first(h,o).start()
            second(h,o).start()
            if wait: to_twin(h,o).start()
    def sides(zz):
        o=chip_of(zz,y,1-x)
        arrived(0,o); to_y(0,o).start(); to_twin(0,o).start()
        o=chip_of(zz,1-y,x)
        arrived(1,o); to_x(1,o).start(); to_twin(1,o).start()
    def both(d,run):
        for zz,up in ((z-d,True),(z+d,False)):
            @pl.when((zz>=0)&(zz<depth))
            def _(): run(zz,up)
    line(z,False,True,True)
    for d in range(1,depth+1):
        if d<depth:
            both(d,lambda zz,up: line(zz,True,up,not up))
        if d==1: sides(z)
        else: both(d-1,lambda zz,up: sides(zz))
    @pl.loop(0,depth)
    def _(zz):
        for a in range(2):
            o=chip_of(zz,1-y,a)
            arrived(0,o); to_twin(0,o).start()
            o=chip_of(zz,a,1-x)
            arrived(1,o); to_twin(1,o).start()
    @pl.loop(1,depth*4)
    def _(k):
        o=lax.rem(me+k,depth*4)
        for h in range(2):
            remote(block(h,o,1-core),block(h,o,1-core),pair_s,twin_r.at[h,o],twin).wait_recv()
            to_twin(h,o).wait_send()
    @pl.loop(0,depth)
    def _(zz):
        o=chip_of(zz,y,x)
        for h in range(2):
            to_x(h,o).wait_send(); to_y(h,o).wait_send()
            @pl.when((z<depth-1)&(zz<=z))
            def _(): to_up(h,o).wait_send()
            @pl.when((z>0)&(zz>=z))
            def _(): to_down(h,o).wait_send()
        to_y(0,chip_of(zz,y,1-x)).wait_send()
        to_x(1,chip_of(zz,1-y,x)).wait_send()

def gather_weights(conv,dense,attn,vec,depth):
    c=conv.shape[2]
    chips=depth*4
    dma=pltpu.SemaphoreType.DMA
    return pl.pallas_call(functools.partial(gather_body,depth),
        out_shape=jax.ShapeDtypeStruct((GATHER,c,c),BF),
        in_specs=[VMEM]*4,out_specs=VMEM,
        scratch_shapes=[pltpu.VMEM((2,GATHER,8,c),F32),pltpu.VMEM((16,c),F32),dma,dma]+[dma((2,chips))]*7,
        compiler_params=pltpu.CompilerParams(collective_id=0,has_side_effects=True,vmem_limit_bytes=LIMIT),
        name="gather_weights")(conv,dense,attn,vec)

REDUCE=MATS+2
HALF=REDUCE//2
PARTS=((0,5,"xyz"),(5,4,"yzx"),(9,3,"zxy"))

def reduce_body(depth, inv_ref, g_ref, v_ref, q_ref, vec_o, acc, core_in, bx0, by0, up0, down0, bx1, by1, up1, down1, bx2, by2, up2, down2,
                final, pick, vsend, vrecv, core_s, core_r, ex_s, ex_r, up_s, up_r, down_s, down_r, twin_s, twin_r, out_s, out_r, v_s, v_r):
    z,y,x,core=place()
    me=chip_of(z,y,x)
    chips=depth*4
    twin=device(z,y,x,1-core)
    def of_chip(o):
        return device(lax.div(o,4),lax.rem(lax.div(o,2),2),lax.rem(o,2),core)
    others=[lax.rem(me+k,chips) for k in range(1,chips)]
    greet([(twin,None)]+[(of_chip(o),None) for o in others])
    c=g_ref.shape[2]
    pair=[]
    for i,(m0,n,_) in enumerate(PARTS):
        cp=remote(g_ref.at[pl.ds(HALF*(1-core)+m0,n)],core_in.at[m0:m0+n],core_s.at[i],core_r.at[i],twin)
        cp.start(); pair.append(cp)
    def vec_start(stage,dev):
        cp=remote(vsend.at[stage],vrecv.at[stage],v_s.at[stage],v_r.at[stage],dev)
        cp.start()
        return cp
    def vec_end(stage,cp):
        cp.wait()
        total=vsend[stage]+vrecv[stage]
        if stage<4: vsend[stage+1]=total
        else: vec_o[...]=total
    vsend[0]=v_ref[...]
    vcp=vec_start(0,twin)
    nbr_x,nbr_y=device(z,y,1-x,core),device(z,1-y,x,core)
    bufs=((bx0,by0,up0,down0),(bx1,by1,up1,down1),(bx2,by2,up2,down2))
    started={}
    def where(i,done):
        return ["z" in done and z, "y" in done and y, "x" in done and x]
    def index(m,place):
        return tuple([m]+[slice(None) if p is False else p for p in place])
    def swap_start(i,stage):
        m0,n,order=PARTS[i]
        axis=order[stage]
        at=where(i,order[:stage])
        at["zyx".index(axis)]=1-(x if axis=="x" else y)
        dst=bufs[i][0 if axis=="x" else 1]
        k=0 if axis=="x" else 1
        cp=remote(acc.at[index(slice(m0,m0+n),at)],dst,ex_s.at[i,k],ex_r.at[i,k],nbr_x if axis=="x" else nbr_y)
        cp.start()
        started[i,stage]=cp
    def swap_end(i,stage):
        m0,n,order=PARTS[i]
        axis=order[stage]
        started.pop((i,stage)).wait()
        at=where(i,order[:stage+1])
        src=bufs[i][0 if axis=="x" else 1]
        @pl.loop(0,n)
        def _(m):
            there=index(m0+m,at)
            acc[there]=(acc[there].astype(F32)+src[m].astype(F32)).astype(BF)
    def z_line(i,stage):
        m0,n,order=PARTS[i]
        at=where(i,order[:stage])
        up,down=bufs[i][2:]
        def view(zz):
            a=list(at); a[0]=zz
            return index(slice(m0,m0+n),a)
        def add(buf,zz):
            a=list(at); a[0]=zz
            @pl.loop(0,n)
            def _(m):
                there=index(m0+m,a)
                acc[there]=(acc[there].astype(F32)+buf[zz,m].astype(F32)).astype(BF)
        def to_up(zz): return remote(acc.at[view(zz)],up.at[zz],up_s.at[i,zz],up_r.at[i,zz],device(z+1,y,x,core))
        def to_down(zz): return remote(acc.at[view(zz)],down.at[zz],down_s.at[i,zz],down_r.at[i,zz],device(z-1,y,x,core))
        for k in range(depth-1):
            top,low=depth-1-k,k
            @pl.when(z<top)
            def _():
                @pl.when(z>0)
                def _():
                    to_up(top).wait_recv(); add(up,top)
                to_up(top).start()
            @pl.when(z>low)
            def _():
                @pl.when(z<depth-1)
                def _():
                    to_down(low).wait_recv(); add(down,low)
                to_down(low).start()
        @pl.when(z>0)
        def _():
            to_up(z).wait_recv(); add(up,z)
        @pl.when(z<depth-1)
        def _():
            to_down(z).wait_recv(); add(down,z)
        for k in range(depth-1):
            top,low=depth-1-k,k
            @pl.when(z<top)
            def _(): to_up(top).wait_send()
            @pl.when(z>low)
            def _(): to_down(low).wait_send()

    def add_pair(i):
        m0,n,_=PARTS[i]
        pair[i].wait()
        @pl.loop(0,n)
        def _(m):
            s=(g_ref[HALF*core+m0+m].astype(F32)+core_in[m0+m].astype(F32)).astype(BF)
            acc[m0+m]=s.reshape(acc.shape[1:])
    add_pair(0); swap_start(0,0)
    add_pair(1); swap_start(1,0)
    add_pair(2)
    vec_end(0,vcp); vcp=vec_start(1,nbr_x)
    z_line(2,0)
    vec_end(1,vcp); vcp=vec_start(2,nbr_y)
    swap_end(0,0); swap_start(0,1)
    swap_start(2,1)
    swap_end(1,0)
    z_line(1,1)
    vec_end(2,vcp); vcp=vec_start(3,device(lax.div(z,2)*2+(1-lax.rem(z,2)),y,x,core))
    swap_start(1,2)
    swap_end(2,1); swap_start(2,2)
    swap_end(0,1)
    z_line(0,2)
    vec_end(3,vcp); vcp=vec_start(4,device(lax.rem(z+2,4),y,x,core))
    swap_end(1,2)
    swap_end(2,2)
    there=pl.ds(HALF*core,HALF)
    for m in range(HALF):
        final[HALF*core+m]=acc[m,z,y,x]
    cp=remote(final.at[there],final.at[there],twin_s,twin_r,twin)
    cp.start(); cp.wait()
    for k in range(chips):
        o=me if k==0 else others[k-1]
        m=jnp.maximum(inv_ref[o*2+core],0)
        pick[k,0]=final[m]
        pick[k,1]=final[REDUCE-1]
        if k:
            remote(pick.at[k],q_ref.at[me],out_s.at[k],out_r.at[me],of_chip(o)).start()
    q_ref[me]=pick[0]
    vec_end(4,vcp)
    for k in range(1,chips):
        o=others[k-1]
        remote(pick.at[k],q_ref.at[o],out_s.at[k],out_r.at[o],of_chip(o)).wait()

def reduce_grads(inv,grads,vec,depth):
    c=grads.shape[2]
    chips=depth*4
    dma=pltpu.SemaphoreType.DMA
    vm=lambda *s: pltpu.VMEM(s,BF)
    bufs=[]
    for _,n,order in PARTS:
        left={"z":depth,"y":2,"x":2}
        shapes={}
        for axis in order:
            del left[axis]
            shapes[axis]=tuple(left[k] for k in "zyx" if k in left)
        bufs+=[vm(n,*shapes["x"],16,c),vm(n,*shapes["y"],16,c),vm(depth,n,*shapes["z"],16,c),vm(depth,n,*shapes["z"],16,c)]
    return pl.pallas_call(functools.partial(reduce_body,depth),
        out_shape=[jax.ShapeDtypeStruct((chips,2,16,c),BF),jax.ShapeDtypeStruct(vec.shape,F32)],
        in_specs=[SMEM,VMEM,VMEM],out_specs=[VMEM,VMEM],
        scratch_shapes=[vm(HALF,depth,2,2,16,c),vm(HALF,c,c)]+bufs+[vm(REDUCE,16,c),vm(chips,2,16,c),
          pltpu.VMEM((5,)+vec.shape,F32),pltpu.VMEM((5,)+vec.shape,F32),
          dma((3,)),dma((3,)),dma((3,2)),dma((3,2)),dma((3,depth)),dma((3,depth)),dma((3,depth)),dma((3,depth)),dma,dma,
          dma((chips,)),dma((chips,)),dma((5,)),dma((5,))],
        compiler_params=pltpu.CompilerParams(collective_id=1,has_side_effects=True,vmem_limit_bytes=LIMIT),
        name="reduce_grads")(inv,grads,vec)

def deal_body(ndev, send_ref, out_ref, s_sem, r_sem):
    w,n=lax.axis_index("wide"),lax.axis_index("narrow")
    width=lax.axis_size("narrow")
    me=w*width+n
    dev=lambda d: (lax.div(d,width),lax.rem(d,width))
    others=[lax.rem(me+k,ndev) for k in range(1,ndev)]
    greet([(dev(d),None) for d in others])
    def copy(k):
        d=others[k]
        return remote(send_ref.at[d],out_ref.at[me],s_sem.at[k],r_sem.at[me],dev(d))
    for k in range(ndev-1): copy(k).start()
    out_ref[me]=send_ref[me]
    for k in range(ndev-1):
        d=others[k]
        remote(send_ref.at[d],out_ref.at[d],s_sem.at[k],r_sem.at[d],dev(d)).wait()

def deal_updates(send):
    ndev=send.shape[0]
    dma=pltpu.SemaphoreType.DMA
    return pl.pallas_call(functools.partial(deal_body,ndev),
        out_shape=jax.ShapeDtypeStruct(send.shape,send.dtype),
        in_specs=[VMEM],out_specs=VMEM,
        scratch_shapes=[dma((ndev,)),dma((ndev,))],
        compiler_params=pltpu.CompilerParams(collective_id=2,has_side_effects=True,vmem_limit_bytes=LIMIT),
        name="deal_updates")(send)

def weights_body(owners_ref, upd_ref, conv_ref, dense_ref, attn_ref, vm_ref, v1_ref, v2_ref, gv_ref,
                 conv_o, dense_o, attn_o, vec_o, convc_o, densec_o, attnc_o, vecc_o, v1_o, v2_o):
    me=lax.axis_index("wide")*lax.axis_size("narrow")+lax.axis_index("narrow")
    c=dense_ref.shape[1]
    def new(master,number,fan):
        u=upd_ref[owners_ref[number]].astype(F32)[0:master.shape[0]]
        return master-fan**-0.5*(u+0.01*master)
    for k in range(conv_ref.shape[0]):
        v=new(conv_ref[k],k+(k>=9),9*c)
        conv_o[k]=v; convc_o[k]=v.astype(BF)
    v=new(dense_ref[...],9,dense_ref.shape[0]*lax.axis_size("wide")*lax.axis_size("narrow"))
    dense_o[...]=v; densec_o[...]=v.astype(BF)
    for k in range(4):
        v=new(attn_ref[k],19+k,c)
        attn_o[k]=v; attnc_o[k]=v.astype(BF)
    cols,rows=vm_ref.shape
    g=pltpu.roll(gv_ref[...],lax.rem(c-me*cols,c),1)[:,0:128].T[0:cols,0:rows]
    corr=1.0-0.5**STEP
    f=0.5*v1_ref[...]+0.5*g
    s=0.5*v2_ref[...]+0.5*g*g
    v=vm_ref[...]-0.2*(f/corr)/(jnp.sqrt(s/corr)+adam_eps)
    vec_o[...]=v; vecc_o[...]=v.astype(BF)
    v1_o[...]=f; v2_o[...]=s

def new_weights(owners,upd,conv,dense,attn,vm,v1,v2,gvec):
    sd=jax.ShapeDtypeStruct
    mains=(conv,dense,attn,vm)
    return pl.pallas_call(weights_body,
        out_shape=[sd(a.shape,F32) for a in mains]+[sd(a.shape,BF) for a in mains]+[sd(v1.shape,F32)]*2,
        in_specs=[SMEM]+[VMEM]*8,out_specs=[VMEM]*10,
        compiler_params=pltpu.CompilerParams(vmem_limit_bytes=LIMIT),
        name="new_weights")(owners,upd,conv,dense,attn,vm,v1,v2,gvec)

def step(depth, images, time_embed, out_cotangent, conv_master, dense_master, attn_master, vector_master, vector_first, vector_second,
         owners, slot_first, slot_second, slot_left_basis, slot_right_basis, slot_left_stat, slot_right_stat):
    batch,side,_,c=images.shape
    ndev=lax.axis_size("wide")*lax.axis_size("narrow")
    flat=lambda a: a.reshape(batch,side*side,c)
    conv=conv_master.reshape((-1,)+conv_master.shape[2:])
    vector,vector_first,vector_second=vector_master.T,vector_first.T,vector_second.T
    if depth:
        w=gather_weights(conv,dense_master,attn_master,vector,depth)
    else:
        gather=lambda a,axis: lax.all_gather(a.astype(BF),AXES,axis=axis,tiled=True)
        dense=jnp.swapaxes(gather(dense_master,0).reshape(c//16,2,16,c),0,1).reshape(2,c,c)
        vec=jnp.pad(gather(vector_master,1),((0,c-vector_master.shape[0]),(0,0)))
        w=jnp.concatenate([gather(conv,1),gather(attn_master,1),dense,vec[None],jnp.zeros((1,c,c),BF)])
    act,igrad,tgrad,grads,gvec,inv=train_images(owners,flat(images),flat(out_cotangent),time_embed,w,side,ndev)
    if depth:
        q,gvec=reduce_grads(inv,grads,gvec,depth)
        q=q.reshape(-1,c)
    else:
        total=lax.optimization_barrier(lax.psum(grads.astype(F32),AXES)).astype(BF)
        gvec=lax.psum(gvec,AXES)
        held=inv[lax.axis_index(AXES)]
        q=jnp.stack([total[jnp.maximum(held,0)].reshape(c//16,16,c),total[MATS+1].reshape(c//16,16,c)],axis=1).reshape(-1,c)
    *slots,send=owner_step(inv,q,slot_first,slot_second,slot_left_basis,slot_right_basis,slot_left_stat,slot_right_stat,ndev)
    if depth:
        upd=deal_updates(send)
        new=new_weights(owners,upd,conv,dense_master,attn_master,vector,vector_first,vector_second,gvec)
    else:
        upd=lax.all_to_all(send,AXES,0,0,tiled=True)
        new=new_weights(owners,upd,conv,dense_master,attn_master,vector,vector_first,vector_second,gvec)
    conv_new,dense_new,attn_new,vec_new,conv_copy,dense_copy,attn_copy,vec_copy,first_new,second_new=new
    return (act.reshape(images.shape),igrad.reshape(images.shape),tgrad,conv_new.reshape(conv_master.shape),dense_new,attn_new,vec_new.T,
            conv_copy.reshape(conv_master.shape),dense_copy,attn_copy,vec_copy.T,first_new.T,second_new.T,*slots)

def solution(mesh):
    rows,both=P(AXES),P(None,AXES)
    taps=P(None,None,AXES)
    depth=4 if (mesh.shape["wide"],mesh.shape["narrow"])==(8,4) else 0
    return jax.shard_map(functools.partial(step,depth),mesh=mesh,
        in_specs=(rows,rows,rows,taps,rows,both,both,both,both,P())+(rows,)*6,
        out_specs=(rows,rows,rows,taps,rows,both,both,taps,rows,both,both,both,both)+(rows,)*6,
        check_vma=False)
```

profile of v0, /device:TPU:0, one launch (start us, length us, event | category | flops | bytes accessed | tf_op | source)
XLA Modules:
  0.0 234.8 jit_solution(16610508705568721846)
XLA Ops:
  0.7 30.7 %gather_weights.1.w_ref = bf16[26,256,256]{2,1,0:T(8,128)(2,1)} custom-call(f32[18,8,256]{2,1,0:T(8,128)} %bitcast.17, f32[16,256]{1,0:T(8,128)} %dense_ref.3, f32[4,8,256]{2,1,0:T(8,128)} %attn_ref.3, f32[8,12]{1,0:T(8,128)} %bitcast.20), custom_call_target="tpu_custom_call" | custom-call | tf_op jit(solution)/shard_map/gather_weights/pallas_call | solution.py:574
  31.3 93.2 %train_images.1 = (bf16[22,256,256]{2,1,0:T(8,128)(2,1)}, f32[22,256,256]{2,1,0:T(8,128)}, f32[22,512]{1,0:T(8,128)}, bf16[24,256,256]{2,1,0:T(8,128)(2,1)}, f32[16,256]{1,0:T(8,128)}, /*index=5*/s32[32]{0:T(128)}) custom-call(s32[23]{0:T(128)} %owners_ref.3, bf16[22,256,256]{2,1,0:T(8,128)(2,1)} %bitcast.15, bf16[22,256,256]{2,1,0:T(8,128)(2,1)} %bitcast.16, ...), custom_call_target="tpu_custom_call" | custom-call | tf_op jit(solution)/shard_map/train_images/pallas_call | solution.py:269
  124.5 58.4 %reduce_grads.1 = (bf16[16,2,16,256]{3,2,1,0:T(8,128)(2,1)}, f32[16,256]{1,0:T(8,128)}) custom-call(s32[32]{0:T(128)} %get-tuple-element.47.inv_ref, bf16[24,256,256]{2,1,0:T(8,128)(2,1)} %get-tuple-element.48.g_ref, f32[16,256]{1,0:T(8,128)} %get-tuple-element.49.v_ref), custom_call_target="tpu_custom_call" | custom-call | tf_op jit(solution)/shard_map/reduce_grads/pallas_call | solution.py:736
  182.9 36.2 %owner_step.1 = (f32[1,512,256]{2,1,0:T(8,128)}, f32[1,512,256]{2,1,0:T(8,128)}, f32[1,512,512]{2,1,0:T(8,128)}, f32[1,256,256]{2,1,0:T(8,128)}, f32[1,512,512]{...) custom-call(s32[32]{0:T(128)} %get-tuple-element.47.inv_ref, bf16[512,256]{1,0:T(8,128)(2,1)} %bitcast.19, ...), custom_call_target="tpu_custom_call" | custom-call | tf_op jit(solution)/shard_map/owner_step/pallas_call | solution.py:429
  219.1 13.4 %deal_updates.1.upd_ref = bf16[32,16,256]{2,1,0:T(8,128)(2,1)} custom-call(bf16[32,16,256]{2,1,0:T(8,128)(2,1)} %get-tuple-element.51.send_ref), custom_call_target="tpu_custom_call" | custom-call | tf_op jit(solution)/shard_map/deal_updates/pallas_call | solution.py:765
  232.5 1.9 new_weights.1
where the time goes:
time: 235 us
  Pallas kernels  234 us (100%)
    pallas_call x1, Pallas kernels, train_images(): pl.pallas_call(functools.partial(train_body, side), grid=(-(-batch // ib)...  93.2 us
    pallas_call x1, Pallas kernels, reduce_grads(): pl.pallas_call(functools.partial(reduce_body, depth), out_shape=[jax.Shap...  58.4 us
    pallas_call x1, Pallas kernels, owner_step(): pl.pallas_call(owner_body, in_specs=[pl.BlockSpec(memory_space=pltpu.SMEM...  36.2 us
    pallas_call x1, Pallas kernels, gather_weights(): pl.pallas_call(functools.partial(gather_body, depth), out_shape=jax.Shape...  30.7 us
    pallas_call x1, Pallas kernels, deal_updates(): pl.pallas_call(functools.partial(deal_body, ndev), out_shape=jax.ShapeDty...  13.4 us

commit v1 on v0

--- a/solution.py
+++ b/solution.py
@@ -24,6 +24,7 @@
 ANY = pl.BlockSpec(memory_space=pl.ANY)
 LIMIT = 56 << 20
 TOGETHER = 6
+DEAL = False
 
 def mm(a,b):
     return lax.dot_general(a,b,(((1,),(0,)),((),())),preferred_element_type=F32)
@@ -354,44 +355,12 @@
                 a[:,hi:]=a[:,hi:]-dot3(q,r,1,0)
             a[:,lo:hi]=q
 
-def soap(nb, grad, ins, outs, update, g_l, g_r):
-    (first,second,left,right,lstat,rstat)=ins
-    first_o,second_o,left_o,right_o,lstat_o,rstat_o=outs
-    c=right.shape[0]
-    big=left.shape[0]
-    g=grad[...]
-    L=left[...]; Rb=right[...]
-    ls=0.95*lstat[...]+0.05*bdot(g,g,1,1)
-    rs=0.95*rstat[...]+0.05*bdot(g,g,0,0)
-    lstat_o[...]=ls; rstat_o[...]=rs
-    ar=nn(rs,Rb)
-    right_o[...]=ar
-    g_r[...]=tn(ar,ar)
-    al=nn(ls,L)
-    left_o[...]=al
-    unit=(lax.broadcasted_iota(jnp.int32,(big,big),0)==lax.broadcasted_iota(jnp.int32,(big,big),1))&(lax.broadcasted_iota(jnp.int32,(big,big),0)>=nb*c)
-    g_l[...]=tn(al,al)+jnp.where(unit,1.0,0.0)
-    corr=1.0-0.5**STEP
-    turned=dot3(dot2(L,g,0,0),Rb,1,0)
-    inside=lax.broadcasted_iota(jnp.int32,(big,c),0)<nb*c
-    moment=jnp.where(inside,0.5*first[...]+0.5*turned,0.0)
-    sec=jnp.where(inside,0.5*second[...]+0.5*turned*turned,0.0)
-    first_o[...]=moment; second_o[...]=sec
-    direction=moment/corr/(jnp.sqrt(sec/corr)+adam_eps)
-    update[...]=dot3(dot3(L,direction,1,0),Rb,1,1)
-    factor_both(left_o,g_l,right_o,g_r)
-
-def owner_body(inv_ref, q_ref, *refs):
-    ins_hbm=refs[0:6]; outs_hbm=refs[6:12]; send_o=refs[12]
-    ins=refs[13:19]; outs=refs[19:25]
-    grad,update,g_l,g_r,in_sem,out_sem=refs[25:]
-    me=lax.axis_index("wide")*lax.axis_size("narrow")+lax.axis_index("narrow")
-    held=inv_ref[me]
-    kind=jnp.where(held<0,0,jnp.where(held==MATS,2,1))
-    c=ins[3].shape[1]; big=ins[2].shape[1]
-    copies_in=[pltpu.make_async_copy(h.at[0],v,in_sem.at[i]) for i,(h,v) in enumerate(zip(ins_hbm,ins))]
-    copies_out=[pltpu.make_async_copy(v,h.at[0],out_sem.at[i]) for i,(h,v) in enumerate(zip(outs_hbm,outs))]
-    for cp in copies_in: cp.start()
+def owned(inv_ref):
+    held=inv_ref[lax.axis_index("wide")*lax.axis_size("narrow")+lax.axis_index("narrow")]
+    return jnp.where(held<0,0,jnp.where(held==MATS,2,1))
+
+def fetch_grad(kind, q_ref, grad):
+    big=grad.shape[0]
     @pl.when(kind==1)
     def _():
         grad[...]=jnp.zeros_like(grad)
@@ -400,15 +369,39 @@
     @pl.when(kind==2)
     def _():
         grad[...]=q_ref[...]
+
+def copies(srcs,dsts,sems):
+    return [pltpu.make_async_copy(a,b,sems.at[i]) for i,(a,b) in enumerate(zip(srcs,dsts))]
+
+def update_body(inv_ref, q_ref, *refs):
+    ins_hbm=refs[0:4]; outs_hbm=refs[4:6]; send_o=refs[6]
+    ins=refs[7:11]; outs=refs[11:13]
+    grad,update,in_sem,out_sem=refs[13:]
+    first,second,left,right=ins
+    kind=owned(inv_ref)
+    c=right.shape[1]; big=left.shape[1]
+    ndev=send_o.shape[0]
+    copies_in=copies([h.at[0] for h in ins_hbm],ins,in_sem)
+    copies_out=copies(outs,[h.at[0] for h in outs_hbm],out_sem)
+    for cp in copies_in: cp.start()
+    fetch_grad(kind,q_ref,grad)
     for cp in copies_in: cp.wait()
-    ndev=send_o.shape[0]
     @pl.when(kind==0)
     def _():
         for o in outs: o[...]=jnp.zeros_like(o)
         send_o[...]=jnp.zeros_like(send_o)
     @pl.when(kind>0)
     def _():
-        soap(kind,grad,ins,outs,update,g_l,g_r)
+        L=left[...]; Rb=right[...]
+        corr=1.0-0.5**STEP
+        turned=dot3(dot2(L,grad[...],0,0),Rb,1,0)
+        inside=lax.broadcasted_iota(jnp.int32,(big,c),0)<kind*c
+        moment=jnp.where(inside,0.5*first[...]+0.5*turned,0.0)
+        sec=jnp.where(inside,0.5*second[...]+0.5*turned*turned,0.0)
+        outs[0][...]=moment; outs[1][...]=sec
+        direction=moment/corr/(jnp.sqrt(sec/corr)+adam_eps)
+        update[...]=dot3(dot3(L,direction,1,0),Rb,1,1)
+    for cp in copies_out: cp.start()
     for size,number in ((c,1),(big,2)):
         @pl.when(kind==number)
         def _():
@@ -417,23 +410,67 @@
                 u=update[r*d:r*d+r]
                 if r<16: u=jnp.concatenate([u,jnp.zeros((16-r,c),F32)],axis=0)
                 send_o[d]=u.astype(BF)
-    for cp in copies_out: cp.start()
     for cp in copies_out: cp.wait()
 
-def owner_step(inv,q,first,second,left,right,lstat,rstat,ndev):
+def basis_body(inv_ref, q_ref, *refs):
+    ins_hbm=refs[0:4]; outs_hbm=refs[4:8]
+    ins=refs[8:12]; outs=refs[12:16]
+    grad,g_l,g_r,in_sem,out_sem=refs[16:]
+    left,right,lstat,rstat=ins
+    left_o,right_o,lstat_o,rstat_o=outs
+    kind=owned(inv_ref)
     c=right.shape[1]; big=left.shape[1]
-    slots=(first,second,left,right,lstat,rstat)
+    copies_in=copies([h.at[0] for h in ins_hbm],ins,in_sem)
+    copies_out=copies(outs,[h.at[0] for h in outs_hbm],out_sem)
+    for cp in copies_in: cp.start()
+    fetch_grad(kind,q_ref,grad)
+    for cp in copies_in: cp.wait()
+    @pl.when(kind==0)
+    def _():
+        for o in outs: o[...]=jnp.zeros_like(o)
+        for cp in copies_out: cp.start()
+    @pl.when(kind>0)
+    def _():
+        g=grad[...]
+        ls=0.95*lstat[...]+0.05*bdot(g,g,1,1)
+        rs=0.95*rstat[...]+0.05*bdot(g,g,0,0)
+        lstat_o[...]=ls; rstat_o[...]=rs
+        for cp in copies_out[2:]: cp.start()
+        ar=nn(rs,right[...])
+        right_o[...]=ar
+        g_r[...]=tn(ar,ar)
+        al=nn(ls,left[...])
+        left_o[...]=al
+        row=lax.broadcasted_iota(jnp.int32,(big,big),0)
+        unit=(row==lax.broadcasted_iota(jnp.int32,(big,big),1))&(row>=kind*c)
+        g_l[...]=tn(al,al)+jnp.where(unit,1.0,0.0)
+        factor_both(left_o,g_l,right_o,g_r)
+        for cp in copies_out[:2]: cp.start()
+    for cp in copies_out: cp.wait()
+
+def owner_call(body,name,inv,q,ins,outs,extra_out,scratch,cost):
     sd=lambda a: jax.ShapeDtypeStruct(a.shape,F32)
-    vm=pl.BlockSpec(memory_space=pltpu.VMEM); hb=pl.BlockSpec(memory_space=pl.ANY)
     buf=lambda a: pltpu.VMEM(a.shape[1:],F32)
-    return pl.pallas_call(owner_body,
-        in_specs=[pl.BlockSpec(memory_space=pltpu.SMEM),vm]+[hb]*6,
-        out_specs=[hb]*6+[vm],
-        out_shape=[sd(a) for a in slots]+[jax.ShapeDtypeStruct((ndev,16,c),BF)],
-        scratch_shapes=[buf(a) for a in slots]*2+[pltpu.VMEM((big,c),BF),pltpu.VMEM((big,c),F32)]+[pltpu.VMEM((big,big),F32),pltpu.VMEM((c,c),F32),
-          pltpu.SemaphoreType.DMA((6,)),pltpu.SemaphoreType.DMA((6,))],
+    dma=pltpu.SemaphoreType.DMA
+    return pl.pallas_call(body,
+        in_specs=[SMEM,VMEM]+[ANY]*len(ins),
+        out_specs=[ANY]*len(outs)+[VMEM]*len(extra_out),
+        out_shape=[sd(a) for a in outs]+extra_out,
+        scratch_shapes=[buf(a) for a in ins]+[buf(a) for a in outs]+scratch+[dma((len(ins),)),dma((len(outs),))],
         compiler_params=pltpu.CompilerParams(vmem_limit_bytes=LIMIT),
-        name="owner_step")(inv,q,*slots)
+        cost_estimate=pl.CostEstimate(flops=cost,bytes_accessed=4<<20,transcendentals=0),
+        name=name)(inv,q,*ins)
+
+def owner_update(inv,q,first,second,left,right,ndev):
+    c=right.shape[1]; big=left.shape[1]
+    return owner_call(update_body,"owner_update",inv,q,(first,second,left,right),(first,second),
+        [jax.ShapeDtypeStruct((ndev,16,c),BF)],[pltpu.VMEM((big,c),BF),pltpu.VMEM((big,c),F32)],4*10**9)
+
+def owner_basis(inv,q,left,right,lstat,rstat):
+    c=right.shape[1]; big=left.shape[1]
+    slots=(left,right,lstat,rstat)
+    return owner_call(basis_body,"owner_basis",inv,q,slots,slots,[],
+        [pltpu.VMEM((big,c),BF),pltpu.VMEM((big,big),F32),pltpu.VMEM((c,c),F32)],3*10**10)
 
 def place():
     w,n=lax.axis_index("wide"),lax.axis_index("narrow")
@@ -467,13 +504,15 @@
 CUT=(SHARE+1)//2
 
 def gather_body(depth, conv_ref, dense_ref, attn_ref, vec_ref, w_ref, part, vbuf,
-                pair_s, pair_r, own_r, twin_r, up_s, down_s, x_s, y_s, twin_s):
+                pair_s, pair_r, line_r, own_r, twin_r, up_s, down_s, x_s, y_s, twin_s):
     z,y,x,core=place()
     me=chip_of(z,y,x)
     rank=me*2+core
+    c=w_ref.shape[-1]
     twin=device(z,y,x,1-core)
-    greet([(twin,None),(device(z,y,1-x,core),None),(device(z,1-y,x,core),None),
-           (device(z-1,y,x,core),z>0),(device(z+1,y,x,core),z<depth-1)])
+    side_x,side_y=device(z,y,1-x,core),device(z,1-y,x,core)
+    above,below=device(z+1,y,x,core),device(z-1,y,x,core)
+    greet([(twin,None),(side_x,None),(side_y,None),(below,z>0),(above,z<depth-1)])
     conv=conv_ref.shape[0]
     part[0,0:conv]=conv_ref[...]
     part[0,conv:MATS]=attn_ref[...]
@@ -490,100 +529,96 @@
     part[0,MATS+3]=mine[8:16]
     swap=remote(part.at[0],part.at[1],pair_s,pair_r,twin)
     swap.start()
-    rows=lambda o: pl.ds(pl.multiple_of(o*16,16),16)
     swap.wait()
     even,odd=core,1-core
-    for m in range(MATS):
-        w_ref[m,rows(me)]=jnp.concatenate([part[even,m],part[odd,m]],axis=0).astype(BF)
+    join=lambda a,b: jnp.concatenate([a,b],axis=0).astype(BF)
+    def fill(m,value):
+        @pl.when(core==m//SHARE)
+        def _(): w_ref[m,z,y,x]=value()
+    for k in range(2):
+        @pl.when(core==k)
+        def _():
+            for m in range(k*SHARE,min((k+1)*SHARE,MATS)):
+                w_ref[m,z,y,x]=join(part[even,m],part[odd,m])
     for h,src in ((0,even),(1,odd)):
-        w_ref[MATS+h,rows(me)]=jnp.concatenate([part[src,MATS],part[src,MATS+1]],axis=0).astype(BF)
-    w_ref[MATS+2,rows(me)]=jnp.concatenate([part[0,MATS+2]+part[1,MATS+2],part[0,MATS+3]+part[1,MATS+3]],axis=0).astype(BF)
-    w_ref[MATS+3,rows(me)]=jnp.zeros((16,w_ref.shape[2]),BF)
-
-    def block(h,o,whose=core):
-        return w_ref.at[pl.ds(SHARE*whose+(0,CUT)[h],(CUT,SHARE-CUT)[h]),rows(o)]
-    def copy(h,o,send,recv,dev):
-        return remote(block(h,o),block(h,o),send,recv.at[h,o],dev)
-    def arrived(h,o):
-        copy(h,o,pair_s,own_r,twin).wait_recv()
-    side_x,side_y=device(z,y,1-x,core),device(z,1-y,x,core)
-    to_x=lambda h,o: copy(h,o,x_s.at[h,o],own_r,side_x)
-    to_y=lambda h,o: copy(h,o,y_s.at[h,o],own_r,side_y)
-    to_twin=lambda h,o: copy(h,o,twin_s.at[h,o],twin_r,twin)
-    to_up=lambda h,o: copy(h,o,up_s.at[h,o],own_r,device(z+1,y,x,core))
-    to_down=lambda h,o: copy(h,o,down_s.at[h,o],own_r,device(z-1,y,x,core))
-
-    def line(zz,wait,up,down):
-        o=chip_of(zz,y,x)
-        for h in range(2):
-            if wait: arrived(h,o)
-            if up:
-                @pl.when(z<depth-1)
-                def _(): to_up(h,o).start()
-            if down:
-                @pl.when(z>0)
-                def _(): to_down(h,o).start()
-            first,second=((to_x,to_y),(to_y,to_x))[h]
-            first(h,o).start()
-            second(h,o).start()
-            if wait: to_twin(h,o).start()
+        fill(MATS+h,lambda: join(part[src,MATS],part[src,MATS+1]))
+    fill(MATS+2,lambda: join(part[0,MATS+2]+part[1,MATS+2],part[0,MATS+3]+part[1,MATS+3]))
+    fill(MATS+3,lambda: jnp.zeros((16,c),BF))
+
+    def mats(h,whose=core):
+        return pl.ds(SHARE*whose+(0,CUT)[h],(CUT,SHARE-CUT)[h])
+    every=pl.ds(SHARE*core,SHARE)
+    def same(at,send,recv,dev):
+        return remote(w_ref.at[at],w_ref.at[at],send,recv,dev)
+    def to_up(zz): return same((every,zz,y,x),up_s.at[zz],line_r.at[zz],above)
+    def to_down(zz): return same((every,zz,y,x),down_s.at[zz],line_r.at[zz],below)
+    def first(h,zz):
+        at=(mats(h),zz,y,x)
+        return (same(at,x_s.at[0,zz],own_r.at[0,0,zz],side_x),same(at,y_s.at[0,zz],own_r.at[1,0,zz],side_y))[h]
+    def second(h,zz):
+        return (same((mats(0),zz,y),y_s.at[1,zz],own_r.at[0,1,zz],side_y),
+                same((mats(1),zz,slice(None),x),x_s.at[1,zz],own_r.at[1,1,zz],side_x))[h]
+    def line(zz,up,down):
+        if up or down:
+            same((every,zz,y,x),up_s.at[zz],line_r.at[zz],twin).wait_recv()
+        if up is not False:
+            @pl.when(z<depth-1)
+            def _(): to_up(zz).start()
+        if down is not False:
+            @pl.when(z>0)
+            def _(): to_down(zz).start()
+        for h in range(2): first(h,zz).start()
     def sides(zz):
-        o=chip_of(zz,y,1-x)
-        arrived(0,o); to_y(0,o).start(); to_twin(0,o).start()
-        o=chip_of(zz,1-y,x)
-        arrived(1,o); to_x(1,o).start(); to_twin(1,o).start()
+        same((mats(0),zz,y,1-x),x_s.at[0,zz],own_r.at[0,0,zz],side_x).wait_recv()
+        second(0,zz).start()
+        same((mats(1),zz,1-y,x),y_s.at[0,zz],own_r.at[1,0,zz],side_y).wait_recv()
+        second(1,zz).start()
     def both(d,run):
         for zz,up in ((z-d,True),(z+d,False)):
             @pl.when((zz>=0)&(zz<depth))
             def _(): run(zz,up)
-    line(z,False,True,True)
+    line(z,None,None)
     for d in range(1,depth+1):
         if d<depth:
-            both(d,lambda zz,up: line(zz,True,up,not up))
+            both(d,lambda zz,up: line(zz,up,not up))
         if d==1: sides(z)
         else: both(d-1,lambda zz,up: sides(zz))
-    @pl.loop(0,depth)
-    def _(zz):
-        for a in range(2):
-            o=chip_of(zz,1-y,a)
-            arrived(0,o); to_twin(0,o).start()
-            o=chip_of(zz,a,1-x)
-            arrived(1,o); to_twin(1,o).start()
-    @pl.loop(1,depth*4)
-    def _(k):
-        o=lax.rem(me+k,depth*4)
-        for h in range(2):
-            remote(block(h,o,1-core),block(h,o,1-core),pair_s,twin_r.at[h,o],twin).wait_recv()
-            to_twin(h,o).wait_send()
-    @pl.loop(0,depth)
-    def _(zz):
-        o=chip_of(zz,y,x)
-        for h in range(2):
-            to_x(h,o).wait_send(); to_y(h,o).wait_send()
-            @pl.when((z<depth-1)&(zz<=z))
-            def _(): to_up(h,o).wait_send()
-            @pl.when((z>0)&(zz>=z))
-            def _(): to_down(h,o).wait_send()
-        to_y(0,chip_of(zz,y,1-x)).wait_send()
-        to_x(1,chip_of(zz,1-y,x)).wait_send()
+    for h in range(2):
+        for zz in range(depth):
+            at=((mats(0),zz,1-y),(mats(1),zz,slice(None),1-x))[h]
+            same(at,twin_s.at[h],own_r.at[h,1,zz],twin).wait_recv()
+        same((mats(h),),twin_s.at[h],twin_r.at[h],twin).start()
+    for h in range(2):
+        same((mats(h,1-core),),twin_s.at[h],twin_r.at[h],twin).wait_recv()
+    for h in range(2):
+        same((mats(h),),twin_s.at[h],twin_r.at[h],twin).wait_send()
+        for zz in range(depth):
+            first(h,zz).wait_send(); second(h,zz).wait_send()
+    for zz in range(depth):
+        @pl.when((z<depth-1)&(zz<=z))
+        def _(): to_up(zz).wait_send()
+        @pl.when((z>0)&(zz>=z))
+        def _(): to_down(zz).wait_send()
 
 def gather_weights(conv,dense,attn,vec,depth):
     c=conv.shape[2]
-    chips=depth*4
     dma=pltpu.SemaphoreType.DMA
+    line=dma((depth,))
     return pl.pallas_call(functools.partial(gather_body,depth),
-        out_shape=jax.ShapeDtypeStruct((GATHER,c,c),BF),
+        out_shape=jax.ShapeDtypeStruct((GATHER,depth,2,2,16,c),BF),
         in_specs=[VMEM]*4,out_specs=VMEM,
-        scratch_shapes=[pltpu.VMEM((2,GATHER,8,c),F32),pltpu.VMEM((16,c),F32),dma,dma]+[dma((2,chips))]*7,
+        scratch_shapes=[pltpu.VMEM((2,GATHER,8,c),F32),pltpu.VMEM((16,c),F32),dma,dma,line,dma((2,2,depth)),dma((2,)),line,line,
+          dma((2,depth)),dma((2,depth)),dma((2,))],
         compiler_params=pltpu.CompilerParams(collective_id=0,has_side_effects=True,vmem_limit_bytes=LIMIT),
-        name="gather_weights")(conv,dense,attn,vec)
+        name="gather_weights")(conv,dense,attn,vec).reshape(GATHER,c,c)
 
 REDUCE=MATS+2
 HALF=REDUCE//2
-PARTS=((0,5,"xyz"),(5,4,"yzx"),(9,3,"zxy"))
-
-def reduce_body(depth, inv_ref, g_ref, v_ref, q_ref, vec_o, acc, core_in, bx0, by0, up0, down0, bx1, by1, up1, down1, bx2, by2, up2, down2,
-                final, pick, vsend, vrecv, core_s, core_r, ex_s, ex_r, up_s, up_r, down_s, down_r, twin_s, twin_r, out_s, out_r, v_s, v_r):
+PARTS=((0,3,"xyz"),(3,2,"yzx"),(5,1,"zxy"),(6,2,"xyz"),(8,2,"yzx"),(10,2,"zxy"))
+
+def reduce_body(depth, inv_ref, g_ref, v_ref, q_ref, vec_o, acc, core_in, *rest):
+    bufs=tuple(zip(*[iter(rest[:3*len(PARTS)])]*3))
+    (final, pick, vsend, vrecv, core_s, core_r, ex_s, ex_r, z_s, z_r, twin_s, twin_r, out_s, out_r, v_s, v_r)=rest[3*len(PARTS):]
     z,y,x,core=place()
     me=chip_of(z,y,x)
     chips=depth*4
@@ -609,7 +644,6 @@
     vsend[0]=v_ref[...]
     vcp=vec_start(0,twin)
     nbr_x,nbr_y=device(z,y,1-x,core),device(z,1-y,x,core)
-    bufs=((bx0,by0,up0,down0),(bx1,by1,up1,down1),(bx2,by2,up2,down2))
     started={}
     def where(i,done):
         return ["z" in done and z, "y" in done and y, "x" in done and x]
@@ -635,47 +669,31 @@
         def _(m):
             there=index(m0+m,at)
             acc[there]=(acc[there].astype(F32)+src[m].astype(F32)).astype(BF)
-    def z_line(i,stage):
+    def z_copy(i,stage,k):
         m0,n,order=PARTS[i]
+        zz=lax.rem(z+k,depth)
         at=where(i,order[:stage])
-        up,down=bufs[i][2:]
-        def view(zz):
-            a=list(at); a[0]=zz
-            return index(slice(m0,m0+n),a)
-        def add(buf,zz):
-            a=list(at); a[0]=zz
-            @pl.loop(0,n)
-            def _(m):
-                there=index(m0+m,a)
-                acc[there]=(acc[there].astype(F32)+buf[zz,m].astype(F32)).astype(BF)
-        def to_up(zz): return remote(acc.at[view(zz)],up.at[zz],up_s.at[i,zz],up_r.at[i,zz],device(z+1,y,x,core))
-        def to_down(zz): return remote(acc.at[view(zz)],down.at[zz],down_s.at[i,zz],down_r.at[i,zz],device(z-1,y,x,core))
-        for k in range(depth-1):
-            top,low=depth-1-k,k
-            @pl.when(z<top)
-            def _():
-                @pl.when(z>0)
-                def _():
-                    to_up(top).wait_recv(); add(up,top)
-                to_up(top).start()
-            @pl.when(z>low)
-            def _():
-                @pl.when(z<depth-1)
-                def _():
-                    to_down(low).wait_recv(); add(down,low)
-                to_down(low).start()
-        @pl.when(z>0)
-        def _():
-            to_up(z).wait_recv(); add(up,z)
-        @pl.when(z<depth-1)
-        def _():
-            to_down(z).wait_recv(); add(down,z)
-        for k in range(depth-1):
-            top,low=depth-1-k,k
-            @pl.when(z<top)
-            def _(): to_up(top).wait_send()
-            @pl.when(z>low)
-            def _(): to_down(low).wait_send()
+        at[0]=zz
+        return remote(acc.at[index(slice(m0,m0+n),at)],bufs[i][2].at[z],z_s.at[i,k],z_r.at[i,z],device(zz,y,x,core))
+    def z_start(i,stage):
+        for k in range(1,depth):
+            z_copy(i,stage,k).start()
+    def z_end(i,stage):
+        m0,n,order=PARTS[i]
+        src=bufs[i][2]
+        at=where(i,order[:stage+1])
+        for k in range(1,depth):
+            zz=lax.rem(z+k,depth)
+            remote(src.at[zz],src.at[zz],z_s.at[i,k],z_r.at[i,zz],twin).wait_recv()
+        @pl.loop(0,n)
+        def _(m):
+            there=index(m0+m,at)
+            total=acc[there].astype(F32)
+            for k in range(1,depth):
+                total=total+src[lax.rem(z+k,depth),m].astype(F32)
+            acc[there]=total.astype(BF)
+        for k in range(1,depth):
+            z_copy(i,stage,k).wait_send()
 
     def add_pair(i):
         m0,n,_=PARTS[i]
@@ -684,24 +702,27 @@
         def _(m):
             s=(g_ref[HALF*core+m0+m].astype(F32)+core_in[m0+m].astype(F32)).astype(BF)
             acc[m0+m]=s.reshape(acc.shape[1:])
-    add_pair(0); swap_start(0,0)
-    add_pair(1); swap_start(1,0)
-    add_pair(2)
+    groups=range(0,len(PARTS),3)
+    for i in groups:
+        add_pair(i+2); z_start(i+2,0)
+        add_pair(i); swap_start(i,0)
+        add_pair(i+1); swap_start(i+1,0)
     vec_end(0,vcp); vcp=vec_start(1,nbr_x)
-    z_line(2,0)
+    for i in groups:
+        swap_end(i,0); swap_start(i,1)
+        swap_end(i+1,0); z_start(i+1,1)
+        z_end(i+2,0); swap_start(i+2,1)
     vec_end(1,vcp); vcp=vec_start(2,nbr_y)
-    swap_end(0,0); swap_start(0,1)
-    swap_start(2,1)
-    swap_end(1,0)
-    z_line(1,1)
+    for i in groups:
+        swap_end(i,1); z_start(i,2)
+        swap_end(i+2,1); swap_start(i+2,2)
+        z_end(i+1,1); swap_start(i+1,2)
     vec_end(2,vcp); vcp=vec_start(3,device(lax.div(z,2)*2+(1-lax.rem(z,2)),y,x,core))
-    swap_start(1,2)
-    swap_end(2,1); swap_start(2,2)
-    swap_end(0,1)
-    z_line(0,2)
+    for i in groups:
+        swap_end(i+2,2)
+        swap_end(i+1,2)
+        z_end(i,2)
     vec_end(3,vcp); vcp=vec_start(4,device(lax.rem(z+2,4),y,x,core))
-    swap_end(1,2)
-    swap_end(2,2)
     there=pl.ds(HALF*core,HALF)
     for m in range(HALF):
         final[HALF*core+m]=acc[m,z,y,x]
@@ -732,13 +753,13 @@
         for axis in order:
             del left[axis]
             shapes[axis]=tuple(left[k] for k in "zyx" if k in left)
-        bufs+=[vm(n,*shapes["x"],16,c),vm(n,*shapes["y"],16,c),vm(depth,n,*shapes["z"],16,c),vm(depth,n,*shapes["z"],16,c)]
+        bufs+=[vm(n,*shapes["x"],16,c),vm(n,*shapes["y"],16,c),vm(depth,n,*shapes["z"],16,c)]
     return pl.pallas_call(functools.partial(reduce_body,depth),
         out_shape=[jax.ShapeDtypeStruct((chips,2,16,c),BF),jax.ShapeDtypeStruct(vec.shape,F32)],
         in_specs=[SMEM,VMEM,VMEM],out_specs=[VMEM,VMEM],
         scratch_shapes=[vm(HALF,depth,2,2,16,c),vm(HALF,c,c)]+bufs+[vm(REDUCE,16,c),vm(chips,2,16,c),
           pltpu.VMEM((5,)+vec.shape,F32),pltpu.VMEM((5,)+vec.shape,F32),
-          dma((3,)),dma((3,)),dma((3,2)),dma((3,2)),dma((3,depth)),dma((3,depth)),dma((3,depth)),dma((3,depth)),dma,dma,
+          dma((len(PARTS),)),dma((len(PARTS),)),dma((len(PARTS),2)),dma((len(PARTS),2)),dma((len(PARTS),depth)),dma((len(PARTS),depth)),dma,dma,
           dma((chips,)),dma((chips,)),dma((5,)),dma((5,))],
         compiler_params=pltpu.CompilerParams(collective_id=1,has_side_effects=True,vmem_limit_bytes=LIMIT),
         name="reduce_grads")(inv,grads,vec)
@@ -825,13 +846,10 @@
         gvec=lax.psum(gvec,AXES)
         held=inv[lax.axis_index(AXES)]
         q=jnp.stack([total[jnp.maximum(held,0)].reshape(c//16,16,c),total[MATS+1].reshape(c//16,16,c)],axis=1).reshape(-1,c)
-    *slots,send=owner_step(inv,q,slot_first,slot_second,slot_left_basis,slot_right_basis,slot_left_stat,slot_right_stat,ndev)
-    if depth:
-        upd=deal_updates(send)
-        new=new_weights(owners,upd,conv,dense_master,attn_master,vector,vector_first,vector_second,gvec)
-    else:
-        upd=lax.all_to_all(send,AXES,0,0,tiled=True)
-        new=new_weights(owners,upd,conv,dense_master,attn_master,vector,vector_first,vector_second,gvec)
+    first_slot,second_slot,send=owner_update(inv,q,slot_first,slot_second,slot_left_basis,slot_right_basis,ndev)
+    upd=deal_updates(send) if depth and DEAL else lax.all_to_all(send,AXES,0,0,tiled=True)
+    slots=[first_slot,second_slot]+list(owner_basis(inv,q,slot_left_basis,slot_right_basis,slot_left_stat,slot_right_stat))
+    new=new_weights(owners,upd,conv,dense_master,attn_master,vector,vector_first,vector_second,gvec)
     conv_new,dense_new,attn_new,vec_new,conv_copy,dense_copy,attn_copy,vec_copy,first_new,second_new=new
     return (act.reshape(images.shape),igrad.reshape(images.shape),tgrad,conv_new.reshape(conv_master.shape),dense_new,attn_new,vec_new.T,
             conv_copy.reshape(conv_master.shape),dense_copy,attn_copy,vec_copy.T,first_new.T,second_new.T,*slots)

time: 235 us -> 206 us (0.88)
  Pallas kernels: 234 us -> 198 us
  starting transfers between devices: 0 us -> 5.58 us
    pallas_call x1, Pallas kernels: 58.4 us -> 36.9 us  [reduce_grads(): pl.pallas_call(functools.partial(reduce_body, depth), out_shape=[jax.Shap...]
    pallas_call x2, Pallas kernels: 49.5 us -> 40.8 us  [owner_call(): pl.pallas_call(body, in_specs=[SMEM, VMEM] + [ANY] * len(ins), out_specs=...]
    pallas_call x1, Pallas kernels: 93.2 us -> 86.8 us  [train_images(): pl.pallas_call(functools.partial(train_body, side), grid=(-(-batch // ib)...]
    all_to_all x0 -> x1, starting transfers between devices: none -> 5.58 us  [step(): lax.all_to_all(send, AXES, 0, 0, tiled=True)]
  transfers between devices with their start and end apart: 0 -> 1, of which waited for: 0 -> 0; matrix products, arithmetic and copies ran while one was open for 0% -> 0% of each run, Pallas kernels for 0% -> 17%
where the time goes in v1:
time: 206 us
  Pallas kernels  198 us (96%)
  starting transfers between devices  5.58 us (3%)
    pallas_call x1, Pallas kernels, train_images(): pl.pallas_call(functools.partial(train_body, side), grid=(-(-batch // ib)...  86.8 us
    pallas_call x2, Pallas kernels, owner_call(): pl.pallas_call(body, in_specs=[SMEM, VMEM] + [ANY] * len(ins), out_specs=...  40.8 us
    pallas_call x1, Pallas kernels, reduce_grads(): pl.pallas_call(functools.partial(reduce_body, depth), out_shape=[jax.Shap...  36.9 us
    pallas_call x1, Pallas kernels, gather_weights(): pl.pallas_call(functools.partial(gather_body, depth), out_shape=jax.Shape...  31.9 us
    all_to_all x1, starting transfers between devices, step(): lax.all_to_all(send, AXES, 0, 0, tiled=True)  5.58 us
  transfers between devices with their start and end apart: 1, of which 0 were waited for; matrix products, arithmetic and copies ran while one was open for 0% of the time, Pallas kernels for 17%

profile of v1, /device:TPU:0, one launch (start us, length us, event | category | flops | bytes accessed | tf_op | source)
XLA Modules:
  0.0 205.7 jit_solution(16462528780102755722)
XLA Ops:
  0.7 31.9 %gather_weights.1 = bf16[26,4,2,2,16,256]{5,4,3,2,1,0:T(8,128)(2,1)} custom-call(f32[18,8,256]{2,1,0:T(8,128)} %bitcast.19, f32[16,256]{1,0:T(8,128)} %dense_ref.3, f32[4,8,256]{2,1,0:T(8,128)} %attn_ref.3, f32[8,12]{1,0:T(8,128)} %bitcast.21), custom_call_target="tpu_custom_call" | custom-call | tf_op jit(solution)/shard_map/gather_weights/pallas_call | solution.py:607
  32.6 86.8 %train_images.1 = (bf16[22,256,256]{2,1,0:T(8,128)(2,1)}, f32[22,256,256]{2,1,0:T(8,128)}, f32[22,512]{1,0:T(8,128)}, bf16[24,256,256]{2,1,0:T(8,128)(2,1)}, f32[16,256]{1,0:T(8,128)}, /*index=5*/s32[32]{0:T(128)}) custom-call(s32[23]{0:T(128)} %owners_ref.3, bf16[22,256,256]{2,1,0:T(8,128)(2,1)} %bitcast.17, bf16[22,256,256]{2,1,0:T(8,128)(2,1)} %bitcast.18, ...), custom_call_target="tpu_custom_call" | custom-call | tf_op jit(solution)/shard_map/train_images/pallas_call | solution.py:270
  119.4 36.9 %reduce_grads.1 = (bf16[16,2,16,256]{3,2,1,0:T(8,128)(2,1)}, f32[16,256]{1,0:T(8,128)}) custom-call(s32[32]{0:T(128)} %get-tuple-element.47.inv_ref, bf16[24,256,256]{2,1,0:T(8,128)(2,1)} %get-tuple-element.48.g_ref, f32[16,256]{1,0:T(8,128)} %get-tuple-element.49.v_ref), custom_call_target="tpu_custom_call" | custom-call | tf_op jit(solution)/shard_map/reduce_grads/pallas_call | solution.py:757
  156.3 6.8 %owner_update.1 = (f32[1,512,256]{2,1,0:T(8,128)}, f32[1,512,256]{2,1,0:T(8,128)}, bf16[32,16,256]{2,1,0:T(8,128)(2,1)}) custom-call(s32[32]{0:T(128)} %get-tuple-element.47.inv_ref, bf16[512,256]{1,0:T(8,128)(2,1)} %bitcast.27, f32[1,512,256]{2,1,0:T(8,128)} %refs_0_.2, f32[1,512,256]{2,1,0:T(8,128)} %refs_1_.2, f32[1,512,512]{2,1,0:T(8,128)} %refs_0_.3, ...), custom_call_target="tpu_custom_call" | custom-call | flops 4000000000 | bytes 4194304 | tf_op jit(solution)/shard_map/owner_update/pallas_call | solution.py:455
  163.0 5.6 %all-to-all-start = ((bf16[32,16,256]{2,1,0:T(8,128)(2,1)}), bf16[32,16,256]{2,1,0:T(8,128)(2,1)S(1)}, u32[]{:S(2)}, u32[]{:S(2)}) async-start(bf16[32,16,256]{2,1,0:T(8,128)(2,1)} %get-tuple-element.51), calls=%async_computation | async-start | bytes 524288 | tf_op jit(solution)/shard_map/all_to_all | solution.py:850
  168.6 34.0 %owner_basis.1 = (f32[1,512,512]{2,1,0:T(8,128)}, f32[1,256,256]{2,1,0:T(8,128)}, f32[1,512,512]{2,1,0:T(8,128)}, f32[1,256,256]{2,1,0:T(8,128)}) custom-call(s32[32]{0:T(128)} %get-tuple-element.47.inv_ref, bf16[512,256]{1,0:T(8,128)(2,1)} %bitcast.28, f32[1,512,512]{2,1,0:T(8,128)} %refs_0_.3, f32[1,256,256]{2,1,0:T(8,128)} %refs_1_.3, ...), custom_call_target="tpu_custom_call" | custom-call | flops 30000001024 | bytes 4194304 | tf_op jit(solution)/shard_map/owner_basis/pallas_call | solution.py:455
  202.7 0.0 all-to-all-done.upd_ref
  202.7 0.0 copy-start
  202.7 0.7 copy-done
  203.4 1.9 new_weights.1
Async XLA Ops:
  163.0 39.6 %all-to-all-start = ((bf16[32,16,256]{2,1,0:T(8,128)(2,1)}), bf16[32,16,256]{2,1,0:T(8,128)(2,1)S(1)}, u32[]{:S(2)}, u32[]{:S(2)}) async-start(bf16[32,16,256]{2,1,0:T(8,128)(2,1)} %get-tuple-element.51), calls=%async_computation | async-start | bytes 524288 | tf_op jit(solution)/shard_map/all_to_all | solution.py:850
  202.7 0.7 copy-start

commit v2 on v1

--- a/solution.py
+++ b/solution.py
@@ -12,6 +12,7 @@
 STEP = 10
 GROUP = 8
 BLK = 128
+ROWS = 256
 half_root = 0.5**0.5
 norm_eps = 1e-6
 adam_eps = 1e-8
@@ -73,12 +74,15 @@
 
 def spread(ref, i, v, side):
     tokens, c = v.shape
-    x=lax.broadcasted_iota(jnp.int32,(tokens,1),0) & (side-1)
-    before=jnp.where(x==0,0.0,pltpu.roll(v,1,0)).astype(BF)
-    after=jnp.where(x==side-1,0.0,pltpu.roll(v,tokens-1,0)).astype(BF)
-    ref[i,side:side+tokens,0:c]=before
+    parts=v.reshape(tokens//16,2,8,c)
+    low,high=parts[:,0],parts[:,1]
+    at=lax.broadcasted_iota(jnp.int32,low.shape,1)
+    whole=lambda a,b: jnp.stack([a,b],axis=1).reshape(tokens,c).astype(BF)
+    l,h=pltpu.roll(low,1,1),pltpu.roll(high,1,1)
+    ref[i,side:side+tokens,0:c]=whole(jnp.where(at==0,0.0,l),jnp.where(at==0,l,h))
     ref[i,side:side+tokens,c:2*c]=v.astype(BF)
-    ref[i,side:side+tokens,2*c:3*c]=after
+    l,h=pltpu.roll(low,7,1),pltpu.roll(high,7,1)
+    ref[i,side:side+tokens,2*c:3*c]=whole(jnp.where(at==7,h,l),jnp.where(at==7,0.0,h))
 
 def taps(ref, count, dy, tokens, side):
     return jnp.concatenate([ref[i,side*dy:side*dy+tokens,:] for i in range(count)],axis=0)
@@ -128,11 +132,8 @@
     def three(ref,k,dy):
         return jnp.concatenate([ref[k+3*dy+dx] for dx in range(3)],axis=0)
     def conv(ref,i,weight):
-        out=None
-        for dy in range(3):
-            part=mm(ref[i,side*dy:side*dy+tokens,:],weight(dy))
-            out=part if out is None else out+part
-            yield
+        out=mm(jnp.concatenate([ref[i,side*dy:side*dy+tokens,:] for dy in range(3)],axis=1),jnp.concatenate([weight(dy) for dy in range(3)],axis=0))
+        yield
         return out
     def wgrad(base,aref,gref,i):
         at=aref[i,side:side+tokens,c:2*c].T
@@ -170,7 +171,7 @@
         sc=mm_nt(q,k)*scale
         yield
         e=jnp.exp(sc-jnp.max(sc,axis=1,keepdims=True))
-        a=e/jnp.sum(e,axis=1,keepdims=True)
+        a=e*pl.reciprocal(jnp.sum(e,axis=1,keepdims=True),approx=True)
         low=a.astype(BF)
         yield
         mixed=mm(low,v).astype(BF)
@@ -282,7 +283,9 @@
 nt=lambda a,b: fdot(a,b,1,1)
 tn=lambda a,b: fdot(a,b,0,0)
 
-def inverse_factors(blocks):
+def inverse_factors(blocks, tasks):
+    tasks=list(tasks)
+    share=-(-len(tasks)//14)
     n=BLK
     lane=lax.broadcasted_iota(jnp.int32,(8,n),1)
     sub=lax.broadcasted_iota(jnp.int32,(8,n),0)
@@ -322,6 +325,7 @@
                 for k in range(8):
                     new=new-over_lanes(t[v],lo+k)*P[k]
                 t[v]=new
+        for _ in range(min(share,len(tasks))): tasks.pop(0)()
     return [jnp.concatenate(t,axis=0) for t in tables]
 
 def at(k,size):
@@ -343,17 +347,31 @@
     return bdot(ah,b,ca,cb)+bdot(al,b,ca,cb)
 
 def factor_both(a_l, g_l, a_r, g_r):
+    tasks=[]
+    def renew(a,lo,inv,r,rows):
+        def task():
+            q=dot3(a[rows,lo:lo+BLK],inv,1,1)
+            a[rows,lo:lo+BLK]=q
+            if r is not None: a[rows,lo+BLK:]=a[rows,lo+BLK:]-dot3(q,r,1,0)
+        return task
+    def lower(g,r,start,b):
+        def task():
+            g[b:b+BLK,b:]=g[b:b+BLK,b:]-tn(r[:,b-start:b-start+BLK],r[:,b-start:])
+        return task
     for p in range(g_l.shape[0]//BLK):
         lo,hi=p*BLK,(p+1)*BLK
         live=[(a,g) for a,g in ((a_l,g_l),(a_r,g_r)) if g.shape[0]>lo]
-        invs=inverse_factors([g[lo:hi,lo:hi] for _,g in live])
+        invs=inverse_factors([g[lo:hi,lo:hi] for _,g in live],tasks)
+        tasks=[]
         for (a,g),inv in zip(live,invs):
-            q=dot3(a[:,lo:hi],inv,1,1)
-            if hi<g.shape[0]:
+            n=g.shape[0]
+            r=None
+            if hi<n:
                 r=nn(inv,g[lo:hi,hi:])
-                g[hi:,hi:]=g[hi:,hi:]-tn(r,r)
-                a[:,hi:]=a[:,hi:]-dot3(q,r,1,0)
-            a[:,lo:hi]=q
+                lower(g,r,hi,hi)()
+                tasks+=[lower(g,r,hi,b) for b in range(hi+BLK,n,BLK)]
+            tasks+=[renew(a,lo,inv,r,slice(k,k+ROWS)) for k in range(0,n,ROWS)]
+    for task in tasks: task()
 
 def owned(inv_ref):
     held=inv_ref[lax.axis_index("wide")*lax.axis_size("narrow")+lax.axis_index("narrow")]
@@ -436,14 +454,14 @@
         rs=0.95*rstat[...]+0.05*bdot(g,g,0,0)
         lstat_o[...]=ls; rstat_o[...]=rs
         for cp in copies_out[2:]: cp.start()
-        ar=nn(rs,right[...])
+        ar=dot3(rs,right[...],1,0)
         right_o[...]=ar
-        g_r[...]=tn(ar,ar)
-        al=nn(ls,left[...])
+        for k in range(0,c,BLK): g_r[k:k+BLK,k:]=tn(ar[:,k:k+BLK],ar[:,k:])
+        al=dot3(ls,left[...],1,0)
         left_o[...]=al
         row=lax.broadcasted_iota(jnp.int32,(big,big),0)
-        unit=(row==lax.broadcasted_iota(jnp.int32,(big,big),1))&(row>=kind*c)
-        g_l[...]=tn(al,al)+jnp.where(unit,1.0,0.0)
+        unit=jnp.where((row==lax.broadcasted_iota(jnp.int32,(big,big),1))&(row>=kind*c),1.0,0.0)
+        for k in range(0,big,BLK): g_l[k:k+BLK,k:]=tn(al[:,k:k+BLK],al[:,k:])+unit[k:k+BLK,k:]
         factor_both(left_o,g_l,right_o,g_r)
         for cp in copies_out[:2]: cp.start()
     for cp in copies_out: cp.wait()

time: 206 us -> 198 us (0.961)
  the two profiles are of different devices: /device:TPU:0 before, /device:TPU:7 now
where the time goes in v2:
time: 198 us; the launch traced here: 197 us
  Pallas kernels  189 us (95%)
  starting transfers between devices  5.96 us (3%)
    pallas_call x1, Pallas kernels, train_images(): pl.pallas_call(functools.partial(train_body, side), grid=(-(-batch // ib)...  82.5 us
    pallas_call x1, Pallas kernels, reduce_grads(): pl.pallas_call(functools.partial(reduce_body, depth), out_shape=[jax.Shap...  37.9 us
    pallas_call x2, Pallas kernels, owner_call(): pl.pallas_call(body, in_specs=[SMEM, VMEM] + [ANY] * len(ins), out_specs=...  37.3 us
    pallas_call x1, Pallas kernels, gather_weights(): pl.pallas_call(functools.partial(gather_body, depth), out_shape=jax.Shape...  29.6 us
    all_to_all x1, starting transfers between devices, step(): lax.all_to_all(send, AXES, 0, 0, tiled=True)  5.96 us
  transfers between devices with their start and end apart: 1, of which 0 were waited for; matrix products, arithmetic and copies ran while one was open for 0% of the time, Pallas kernels for 15%

profile of v2, /device:TPU:7, one launch (start us, length us, event | category | flops | bytes accessed | tf_op | source)
XLA Modules:
  0.0 197.0 jit_solution(4576670856049021257)
XLA Ops:
  0.7 29.6 %gather_weights.1 = bf16[26,4,2,2,16,256]{5,4,3,2,1,0:T(8,128)(2,1)} custom-call(f32[18,8,256]{2,1,0:T(8,128)} %bitcast.19, f32[16,256]{1,0:T(8,128)} %dense_ref.3, f32[4,8,256]{2,1,0:T(8,128)} %attn_ref.3, f32[8,12]{1,0:T(8,128)} %bitcast.21), custom_call_target="tpu_custom_call" | custom-call | tf_op jit(solution)/shard_map/gather_weights/pallas_call | solution.py:625
  30.2 82.5 %train_images.1 = (bf16[22,256,256]{2,1,0:T(8,128)(2,1)}, f32[22,256,256]{2,1,0:T(8,128)}, f32[22,512]{1,0:T(8,128)}, bf16[24,256,256]{2,1,0:T(8,128)(2,1)}, f32[16,256]{1,0:T(8,128)}, /*index=5*/s32[32]{0:T(128)}) custom-call(s32[23]{0:T(128)} %owners_ref.3, bf16[22,256,256]{2,1,0:T(8,128)(2,1)} %bitcast.17, bf16[22,256,256]{2,1,0:T(8,128)(2,1)} %bitcast.18, ...), custom_call_target="tpu_custom_call" | custom-call | tf_op jit(solution)/shard_map/train_images/pallas_call | solution.py:271
  112.7 37.9 %reduce_grads.1 = (bf16[16,2,16,256]{3,2,1,0:T(8,128)(2,1)}, f32[16,256]{1,0:T(8,128)}) custom-call(s32[32]{0:T(128)} %get-tuple-element.47.inv_ref, bf16[24,256,256]{2,1,0:T(8,128)(2,1)} %get-tuple-element.48.g_ref, f32[16,256]{1,0:T(8,128)} %get-tuple-element.49.v_ref), custom_call_target="tpu_custom_call" | custom-call | tf_op jit(solution)/shard_map/reduce_grads/pallas_call | solution.py:775
  150.6 6.8 %owner_update.1 = (f32[1,512,256]{2,1,0:T(8,128)}, f32[1,512,256]{2,1,0:T(8,128)}, bf16[32,16,256]{2,1,0:T(8,128)(2,1)}) custom-call(s32[32]{0:T(128)} %get-tuple-element.47.inv_ref, bf16[512,256]{1,0:T(8,128)(2,1)} %bitcast.27, f32[1,512,256]{2,1,0:T(8,128)} %refs_0_.2, f32[1,512,256]{2,1,0:T(8,128)} %refs_1_.2, f32[1,512,512]{2,1,0:T(8,128)} %refs_0_.3, ...), custom_call_target="tpu_custom_call" | custom-call | flops 4000000000 | bytes 4194304 | tf_op jit(solution)/shard_map/owner_update/pallas_call | solution.py:473
  157.4 6.0 %all-to-all-start = ((bf16[32,16,256]{2,1,0:T(8,128)(2,1)}), bf16[32,16,256]{2,1,0:T(8,128)(2,1)S(1)}, u32[]{:S(2)}, u32[]{:S(2)}) async-start(bf16[32,16,256]{2,1,0:T(8,128)(2,1)} %get-tuple-element.51), calls=%async_computation | async-start | bytes 524288 | tf_op jit(solution)/shard_map/all_to_all | solution.py:868
  163.4 30.5 %owner_basis.1 = (f32[1,512,512]{2,1,0:T(8,128)}, f32[1,256,256]{2,1,0:T(8,128)}, f32[1,512,512]{2,1,0:T(8,128)}, f32[1,256,256]{2,1,0:T(8,128)}) custom-call(s32[32]{0:T(128)} %get-tuple-element.47.inv_ref, bf16[512,256]{1,0:T(8,128)(2,1)} %bitcast.28, f32[1,512,512]{2,1,0:T(8,128)} %refs_0_.3, f32[1,256,256]{2,1,0:T(8,128)} %refs_1_.3, ...), custom_call_target="tpu_custom_call" | custom-call | flops 30000001024 | bytes 4194304 | tf_op jit(solution)/shard_map/owner_basis/pallas_call | solution.py:473
  193.9 0.0 all-to-all-done.upd_ref
  193.9 0.0 copy-start
  193.9 0.7 copy-done
  194.6 1.9 new_weights.1
Async XLA Ops:
  157.4 36.5 %all-to-all-start = ((bf16[32,16,256]{2,1,0:T(8,128)(2,1)}), bf16[32,16,256]{2,1,0:T(8,128)(2,1)S(1)}, u32[]{:S(2)}, u32[]{:S(2)}) async-start(bf16[32,16,256]{2,1,0:T(8,128)(2,1)} %get-tuple-element.51), calls=%async_computation | async-start | bytes 524288 | tf_op jit(solution)/shard_map/all_to_all | solution.py:868
  193.9 0.7 copy-start

commit v3 on v2

--- a/solution.py
+++ b/solution.py
@@ -475,7 +475,7 @@
         out_specs=[ANY]*len(outs)+[VMEM]*len(extra_out),
         out_shape=[sd(a) for a in outs]+extra_out,
         scratch_shapes=[buf(a) for a in ins]+[buf(a) for a in outs]+scratch+[dma((len(ins),)),dma((len(outs),))],
-        compiler_params=pltpu.CompilerParams(vmem_limit_bytes=LIMIT),
+        compiler_params=pltpu.CompilerParams(vmem_limit_bytes=24<<20),
         cost_estimate=pl.CostEstimate(flops=cost,bytes_accessed=4<<20,transcendentals=0),
         name=name)(inv,q,*ins)
 
@@ -779,7 +779,7 @@
           pltpu.VMEM((5,)+vec.shape,F32),pltpu.VMEM((5,)+vec.shape,F32),
           dma((len(PARTS),)),dma((len(PARTS),)),dma((len(PARTS),2)),dma((len(PARTS),2)),dma((len(PARTS),depth)),dma((len(PARTS),depth)),dma,dma,
           dma((chips,)),dma((chips,)),dma((5,)),dma((5,))],
-        compiler_params=pltpu.CompilerParams(collective_id=1,has_side_effects=True,vmem_limit_bytes=LIMIT),
+        compiler_params=pltpu.CompilerParams(collective_id=1,has_side_effects=True,vmem_limit_bytes=18<<20),
         name="reduce_grads")(inv,grads,vec)
 
 def deal_body(ndev, send_ref, out_ref, s_sem, r_sem):
@@ -805,7 +805,7 @@
         out_shape=jax.ShapeDtypeStruct(send.shape,send.dtype),
         in_specs=[VMEM],out_specs=VMEM,
         scratch_shapes=[dma((ndev,)),dma((ndev,))],
-        compiler_params=pltpu.CompilerParams(collective_id=2,has_side_effects=True,vmem_limit_bytes=LIMIT),
+        compiler_params=pltpu.CompilerParams(collective_id=2,has_side_effects=True,vmem_limit_bytes=4<<20),
         name="deal_updates")(send)
 
 def weights_body(owners_ref, upd_ref, conv_ref, dense_ref, attn_ref, vm_ref, v1_ref, v2_ref, gv_ref,
@@ -838,7 +838,7 @@
     return pl.pallas_call(weights_body,
         out_shape=[sd(a.shape,F32) for a in mains]+[sd(a.shape,BF) for a in mains]+[sd(v1.shape,F32)]*2,
         in_specs=[SMEM]+[VMEM]*8,out_specs=[VMEM]*10,
-        compiler_params=pltpu.CompilerParams(vmem_limit_bytes=LIMIT),
+        compiler_params=pltpu.CompilerParams(vmem_limit_bytes=4<<20),
         name="new_weights")(owners,upd,conv,dense,attn,vm,v1,v2,gvec)
 
 def step(depth, images, time_embed, out_cotangent, conv_master, dense_master, attn_master, vector_master, vector_first, vector_second,

time: 198 us -> 195 us (0.985)
  the two profiles are of different devices: /device:TPU:7 before, /device:TPU:0 now
where the time goes in v3:
time: 195 us
  Pallas kernels  184 us (94%)
  starting transfers between devices  5.59 us (3%)
  local copies, waits for them, and re-layouts  3.35 us (2%)
    pallas_call x1, Pallas kernels, train_images(): pl.pallas_call(functools.partial(train_body, side), grid=(-(-batch // ib)...  82.8 us
    pallas_call x1, Pallas kernels, reduce_grads(): pl.pallas_call(functools.partial(reduce_body, depth), out_shape=[jax.Shap...  34.8 us
    pallas_call x2, Pallas kernels, owner_call(): pl.pallas_call(body, in_specs=[SMEM, VMEM] + [ANY] * len(ins), out_specs=...  33.6 us
    pallas_call x1, Pallas kernels, gather_weights(): pl.pallas_call(functools.partial(gather_body, depth), out_shape=jax.Shape...  31.9 us
    all_to_all x1, starting transfers between devices, step(): lax.all_to_all(send, AXES, 0, 0, tiled=True)  5.59 us
  transfers between devices with their start and end apart: 1, of which 0 were waited for; matrix products, arithmetic and copies ran while one was open for 0% of the time, Pallas kernels for 15%

profile of v3, /device:TPU:0, one launch (start us, length us, event | category | flops | bytes accessed | tf_op | source)
XLA Modules:
  0.0 194.8 jit_solution(9766831984273290859)
XLA Ops:
  0.7 31.9 %gather_weights.1 = bf16[26,4,2,2,16,256]{5,4,3,2,1,0:T(8,128)(2,1)} custom-call(f32[18,8,256]{2,1,0:T(8,128)} %bitcast.16, f32[16,256]{1,0:T(8,128)} %dense_ref.3, f32[4,8,256]{2,1,0:T(8,128)} %attn_ref.3, f32[8,12]{1,0:T(8,128)} %bitcast.18), custom_call_target="tpu_custom_call" | custom-call | tf_op jit(solution)/shard_map/gather_weights/pallas_call | solution.py:625
  32.6 0.0 copy-start.11
  32.6 0.0 copy-start.13
  32.6 0.0 copy-start.14
  32.6 0.0 copy-start.15
  32.6 82.8 %train_images.1 = (bf16[22,256,256]{2,1,0:T(8,128)(2,1)}, f32[22,256,256]{2,1,0:T(8,128)}, f32[22,512]{1,0:T(8,128)}, bf16[24,256,256]{2,1,0:T(8,128)(2,1)}, f32[16,256]{1,0:T(8,128)}, /*index=5*/s32[32]{0:T(128)}) custom-call(s32[23]{0:T(128)} %owners_ref.3, bf16[22,256,256]{2,1,0:T(8,128)(2,1)} %bitcast.25, bf16[22,256,256]{2,1,0:T(8,128)(2,1)} %bitcast.26, ...), custom_call_target="tpu_custom_call" | custom-call | tf_op jit(solution)/shard_map/train_images/pallas_call | solution.py:271
  115.4 0.0 copy-start.10
  115.4 0.0 copy-start
  115.4 1.9 copy-done
  117.3 0.0 copy-start.4
  117.3 0.7 copy-done.4
  118.0 0.0 copy-start.9
  118.0 0.7 copy-done.9
  118.7 34.8 %reduce_grads.1 = (bf16[16,2,16,256]{3,2,1,0:T(8,128)(2,1)S(1)}, f32[16,256]{1,0:T(8,128)S(1)}) custom-call(s32[32]{0:T(128)S(1)} %copy-done.9, bf16[24,256,256]{2,1,0:T(8,128)(2,1)S(1)} %copy-done, f32[16,256]{1,0:T(8,128)S(1)} %copy-done.4), custom_call_target="tpu_custom_call" | custom-call | tf_op jit(solution)/shard_map/reduce_grads/pallas_call | solution.py:775
  153.5 0.0 copy-done.11
  153.5 0.0 copy-done.13
  153.5 0.0 copy-done.14
  153.5 0.0 copy-done.15
  153.5 0.0 copy-done.10
  153.5 0.0 copy-start.12
  153.5 0.0 copy-start.16
  153.6 5.0 %owner_update.1 = (f32[1,512,256]{2,1,0:T(8,128)}, f32[1,512,256]{2,1,0:T(8,128)}, bf16[32,16,256]{2,1,0:T(8,128)(2,1)}) custom-call(s32[32]{0:T(128)S(1)} %copy-done.10, bf16[512,256]{1,0:T(8,128)(2,1)S(1)} %bitcast.22, f32[1,512,256]{2,1,0:T(8,128)S(1)} %copy-done.13, f32[1,512,256]{2,1,0:T(8,128)S(1)} %copy-done.14, f32[1,512,512]{2,1,0:T(8,128)S(1)} %copy-done.11, ...), custom_call_target="tpu_custom_call" | custom-call | flops 4000000000 | bytes 4194304 | tf_op jit(solution)/shard_map/owner_update/pallas_call | solution.py:473
  158.5 5.6 %all-to-all-start = ((bf16[32,16,256]{2,1,0:T(8,128)(2,1)}), bf16[32,16,256]{2,1,0:T(8,128)(2,1)S(1)}, u32[]{:S(2)}, u32[]{:S(2)}) async-start(bf16[32,16,256]{2,1,0:T(8,128)(2,1)} %get-tuple-element.51), calls=%async_computation | async-start | bytes 524288 | tf_op jit(solution)/shard_map/all_to_all | solution.py:868
  164.1 0.0 copy-done.12
  164.1 0.0 copy-done.16
  164.2 0.0 copy-start.1
  164.2 0.0 copy-start.2
  164.2 0.0 copy-start.3
  164.2 0.0 copy-start.5
  164.2 0.0 copy-start.6
  164.2 0.0 copy-start.7
  164.2 0.0 copy-start.8
  164.2 28.7 %owner_basis.1 = (f32[1,512,512]{2,1,0:T(8,128)}, f32[1,256,256]{2,1,0:T(8,128)}, f32[1,512,512]{2,1,0:T(8,128)}, f32[1,256,256]{2,1,0:T(8,128)}) custom-call(s32[32]{0:T(128)S(1)} %copy-done.10, bf16[512,256]{1,0:T(8,128)(2,1)S(1)} %bitcast.23, f32[1,512,512]{2,1,0:T(8,128)S(1)} %copy-done.11, f32[1,256,256]{2,1,0:T(8,128)S(1)} %copy-done.15, ...), custom_call_target="tpu_custom_call" | custom-call | flops 30000001024 | bytes 4194304 | tf_op jit(solution)/shard_map/owner_basis/pallas_call | solution.py:473
  192.9 0.0 all-to-all-done.upd_ref
  192.9 0.0 copy-done.1
  192.9 0.0 copy-done.2
  192.9 0.0 copy-done.3
  192.9 0.0 copy-done.5
  193.0 0.0 copy-done.6
  193.0 0.0 copy-done.7
  193.0 0.0 copy-done.8
  193.0 1.4 new_weights.1
Async XLA Ops:
  32.6 120.9 %copy-start.11 = (f32[1,512,512]{2,1,0:T(8,128)S(1)}, f32[1,512,512]{2,1,0:T(8,128)}, u32[]{:S(2)}) copy-start(f32[1,512,512]{2,1,0:T(8,128)} %refs_0_.3) | copy-start | bytes 3145732
  32.6 120.9 %copy-start.13 = (f32[1,512,256]{2,1,0:T(8,128)S(1)}, f32[1,512,256]{2,1,0:T(8,128)}, u32[]{:S(2)}) copy-start(f32[1,512,256]{2,1,0:T(8,128)} %refs_0_.2) | copy-start | bytes 1572868
  32.6 120.9 %copy-start.14 = (f32[1,512,256]{2,1,0:T(8,128)S(1)}, f32[1,512,256]{2,1,0:T(8,128)}, u32[]{:S(2)}) copy-start(f32[1,512,256]{2,1,0:T(8,128)} %refs_1_.2) | copy-start | bytes 1572868
  32.6 120.9 %copy-start.15 = (f32[1,256,256]{2,1,0:T(8,128)S(1)}, f32[1,256,256]{2,1,0:T(8,128)}, u32[]{:S(2)}) copy-start(f32[1,256,256]{2,1,0:T(8,128)} %refs_1_.3) | copy-start | bytes 786436
  115.4 38.1 %copy-start.10 = (s32[32]{0:T(128)S(1)}, s32[32]{0:T(128)}, u32[]{:S(2)}) copy-start(s32[32]{0:T(128)} %get-tuple-element.47.inv_ref) | copy-start | bytes 388
  115.4 1.9 copy-start
  117.3 0.7 copy-start.4
  118.0 0.7 copy-start.9
  153.5 10.6 %copy-start.12 = (f32[1,512,512]{2,1,0:T(8,128)S(1)}, f32[1,512,512]{2,1,0:T(8,128)}, u32[]{:S(2)}) copy-start(f32[1,512,512]{2,1,0:T(8,128)} %refs_2_.3) | copy-start | bytes 3145732
  153.5 10.6 %copy-start.16 = (f32[1,256,256]{2,1,0:T(8,128)S(1)}, f32[1,256,256]{2,1,0:T(8,128)}, u32[]{:S(2)}) copy-start(f32[1,256,256]{2,1,0:T(8,128)} %refs_3_.3) | copy-start | bytes 786436
  158.5 34.4 %all-to-all-start = ((bf16[32,16,256]{2,1,0:T(8,128)(2,1)}), bf16[32,16,256]{2,1,0:T(8,128)(2,1)S(1)}, u32[]{:S(2)}, u32[]{:S(2)}) async-start(bf16[32,16,256]{2,1,0:T(8,128)(2,1)} %get-tuple-element.51), calls=%async_computation | async-start | bytes 524288 | tf_op jit(solution)/shard_map/all_to_all | solution.py:868
  164.2 28.8 %copy-start.1 = (f32[2,9,8,256]{3,2,1,0:T(8,128)S(1)}, f32[2,9,8,256]{3,2,1,0:T(8,128)}, u32[]{:S(2)}) copy-start(f32[2,9,8,256]{3,2,1,0:T(8,128)} %param.19) | copy-start | bytes 442372
  164.2 28.8 %copy-start.2 = (f32[4,8,256]{2,1,0:T(8,128)S(1)}, f32[4,8,256]{2,1,0:T(8,128)}, u32[]{:S(2)}) copy-start(f32[4,8,256]{2,1,0:T(8,128)} %attn_ref.3) | copy-start | bytes 98308
  164.2 28.8 %copy-start.3 = (f32[16,256]{1,0:T(8,128)S(1)}, f32[16,256]{1,0:T(8,128)}, u32[]{:S(2)}) copy-start(f32[16,256]{1,0:T(8,128)} %dense_ref.3) | copy-start | bytes 49156
  164.2 28.8 %copy-start.5 = (f32[12,8]{0,1:T(8,128)S(1)}, f32[12,8]{0,1:T(8,128)}, u32[]{:S(2)}) copy-start(f32[12,8]{0,1:T(8,128)} %param.22) | copy-start | bytes 1156
  164.2 28.8 %copy-start.6 = (f32[12,8]{0,1:T(8,128)S(1)}, f32[12,8]{0,1:T(8,128)}, u32[]{:S(2)}) copy-start(f32[12,8]{0,1:T(8,128)} %param.23) | copy-start | bytes 1156
  164.2 28.8 %copy-start.7 = (f32[12,8]{0,1:T(8,128)S(1)}, f32[12,8]{0,1:T(8,128)}, u32[]{:S(2)}) copy-start(f32[12,8]{0,1:T(8,128)} %param.24) | copy-start | bytes 1156
  164.2 28.8 %copy-start.8 = (s32[23]{0:T(128)S(1)}, s32[23]{0:T(128)}, u32[]{:S(2)}) copy-start(s32[23]{0:T(128)} %owners_ref.3) | copy-start | bytes 280

commit v4 on v3

--- a/solution.py
+++ b/solution.py
@@ -89,7 +89,7 @@
 
 def train_body(side, owners_ref, img_ref, cot_ref, emb_ref, w_ref,
          act_ref, igrad_ref, tgrad_ref, gw_ref, gvec_ref, inv_ref,
-         dense_ref, vec_ref, wt, acc, gvec, proj, pgrad, p1, p2, s2, s1):
+         dense_ref, vec_ref, acc, gvec, proj, pgrad, p1, p2, s2, s1):
     step=pl.program_id(0); steps=pl.num_programs(0)
     ib,tokens,c=img_ref.shape
     batch=emb_ref.shape[0]
@@ -105,9 +105,6 @@
                 z=jnp.zeros((side,3*c),BF)
                 ref[i,0:side,:]=z
                 ref[i,side+tokens:2*side+tokens,:]=z
-        for k in range(2):
-            for t in range(9):
-                wt[k, 8-t]=w_ref[9*k+t].T
         chips=c//16
         total=jnp.zeros((16,c),F32)
         for o in range(chips):
@@ -135,6 +132,10 @@
         out=mm(jnp.concatenate([ref[i,side*dy:side*dy+tokens,:] for dy in range(3)],axis=1),jnp.concatenate([weight(dy) for dy in range(3)],axis=0))
         yield
         return out
+    def back(ref,i,base):
+        out=mm_nt(jnp.concatenate([ref[i,side*dy:side*dy+tokens,:] for dy in range(3)],axis=1),jnp.concatenate([w_ref[base+8-t] for t in range(9)],axis=1))
+        yield
+        return out
     def wgrad(base,aref,gref,i):
         at=aref[i,side:side+tokens,c:2*c].T
         for dy in range(3):
@@ -206,7 +207,7 @@
         add(8,col_sum(g))
         spread(s2,i,g,side)
         yield
-        ag=yield from conv(s2,i,lambda dy: three(wt.at[1],0,dy))
+        ag=yield from back(s2,i,9)
         d=swish_back(ag,h1,row(1),row(4))
         yield
         yield from wgrad(9,p2,s2,i)
@@ -220,7 +221,7 @@
         add(7,pgr)
         spread(s1,i,g,side)
         yield
-        ag=yield from conv(s1,i,lambda dy: three(wt.at[0],0,dy))
+        ag=yield from back(s1,i,0)
         d=swish_back(ag,h0,row(0),row(3))
         yield
         yield from wgrad(0,p1,s1,i)
@@ -272,7 +273,7 @@
         in_specs=[SMEM,blk,blk,whole(embed),whole(w)],
         out_specs=[blk,blk]+[whole(o) for o in outs[2:]]+[SMEM],
         out_shape=outs+[sd((ndev,),jnp.int32)],
-        scratch_shapes=[pltpu.VMEM((emb,c),BF),pltpu.VMEM((16,c),F32),pltpu.VMEM((2,9,c,c),BF),pltpu.VMEM((MATS,c,c),F32),pltpu.VMEM((16,c),F32),pltpu.VMEM((rows,c),F32),pltpu.VMEM((rows,c),F32)]
+        scratch_shapes=[pltpu.VMEM((emb,c),BF),pltpu.VMEM((16,c),F32),pltpu.VMEM((MATS,c,c),F32),pltpu.VMEM((16,c),F32),pltpu.VMEM((rows,c),F32),pltpu.VMEM((rows,c),F32)]
           +[pltpu.VMEM((ib,tokens+2*side,3*c),BF)]*4,
         compiler_params=pltpu.CompilerParams(vmem_limit_bytes=LIMIT),
         name="train_images")(owners,images,cot,embed,w)

time: 195 us -> 190 us (0.974)
  the two profiles are of different devices: /device:TPU:0 before, /device:TPU:3 now
where the time goes in v4:
time: 190 us; the launch traced here: 189 us
  Pallas kernels  180 us (95%)
  starting transfers between devices  4.66 us (2%)
  local copies, waits for them, and re-layouts  3.35 us (2%)
    pallas_call x1, Pallas kernels, train_images(): pl.pallas_call(functools.partial(train_body, side), grid=(-(-batch // ib)...  79.1 us
    pallas_call x1, Pallas kernels, reduce_grads(): pl.pallas_call(functools.partial(reduce_body, depth), out_shape=[jax.Shap...  34.8 us
    pallas_call x2, Pallas kernels, owner_call(): pl.pallas_call(body, in_specs=[SMEM, VMEM] + [ANY] * len(ins), out_specs=...  33.6 us
    pallas_call x1, Pallas kernels, gather_weights(): pl.pallas_call(functools.partial(gather_body, depth), out_shape=jax.Shape...  30.8 us
    all_to_all x1, starting transfers between devices, step(): lax.all_to_all(send, AXES, 0, 0, tiled=True)  4.66 us
  transfers between devices with their start and end apart: 1, of which 0 were waited for; matrix products, arithmetic and copies ran while one was open for 0% of the time, Pallas kernels for 15%

profile of v4, /device:TPU:3, one launch (start us, length us, event | category | flops | bytes accessed | tf_op | source)
XLA Modules:
  0.0 188.9 jit_solution(13788483826229399768)
XLA Ops:
  0.7 30.8 %gather_weights.1 = bf16[26,4,2,2,16,256]{5,4,3,2,1,0:T(8,128)(2,1)} custom-call(f32[18,8,256]{2,1,0:T(8,128)} %bitcast.16, f32[16,256]{1,0:T(8,128)} %dense_ref.3, f32[4,8,256]{2,1,0:T(8,128)} %attn_ref.3, f32[8,12]{1,0:T(8,128)} %bitcast.18), custom_call_target="tpu_custom_call" | custom-call | tf_op jit(solution)/shard_map/gather_weights/pallas_call | solution.py:626
  31.4 0.0 copy-start.11
  31.4 0.0 copy-start.13
  31.5 0.0 copy-start.14
  31.5 0.0 copy-start.15
  31.5 79.1 %train_images.1 = (bf16[22,256,256]{2,1,0:T(8,128)(2,1)}, f32[22,256,256]{2,1,0:T(8,128)}, f32[22,512]{1,0:T(8,128)}, bf16[24,256,256]{2,1,0:T(8,128)(2,1)}, f32[16,256]{1,0:T(8,128)}, /*index=5*/s32[32]{0:T(128)}) custom-call(s32[23]{0:T(128)} %owners_ref.3, bf16[22,256,256]{2,1,0:T(8,128)(2,1)} %bitcast.25, bf16[22,256,256]{2,1,0:T(8,128)(2,1)} %bitcast.26, ...), custom_call_target="tpu_custom_call" | custom-call | tf_op jit(solution)/shard_map/train_images/pallas_call | solution.py:272
  110.6 0.0 copy-start.10
  110.6 0.0 copy-start
  110.6 1.9 copy-done
  112.5 0.0 copy-start.4
  112.5 0.7 copy-done.4
  113.2 0.0 copy-start.9
  113.2 0.7 copy-done.9
  113.9 34.8 %reduce_grads.1 = (bf16[16,2,16,256]{3,2,1,0:T(8,128)(2,1)S(1)}, f32[16,256]{1,0:T(8,128)S(1)}) custom-call(s32[32]{0:T(128)S(1)} %copy-done.9, bf16[24,256,256]{2,1,0:T(8,128)(2,1)S(1)} %copy-done, f32[16,256]{1,0:T(8,128)S(1)} %copy-done.4), custom_call_target="tpu_custom_call" | custom-call | tf_op jit(solution)/shard_map/reduce_grads/pallas_call | solution.py:776
  148.7 0.0 copy-done.11
  148.7 0.0 copy-done.13
  148.7 0.0 copy-done.14
  148.7 0.0 copy-done.15
  148.7 0.0 copy-done.10
  148.7 0.0 copy-start.12
  148.7 0.0 copy-start.16
  148.7 5.0 %owner_update.1 = (f32[1,512,256]{2,1,0:T(8,128)}, f32[1,512,256]{2,1,0:T(8,128)}, bf16[32,16,256]{2,1,0:T(8,128)(2,1)}) custom-call(s32[32]{0:T(128)S(1)} %copy-done.10, bf16[512,256]{1,0:T(8,128)(2,1)S(1)} %bitcast.22, f32[1,512,256]{2,1,0:T(8,128)S(1)} %copy-done.13, f32[1,512,256]{2,1,0:T(8,128)S(1)} %copy-done.14, f32[1,512,512]{2,1,0:T(8,128)S(1)} %copy-done.11, ...), custom_call_target="tpu_custom_call" | custom-call | flops 4000000000 | bytes 4194304 | tf_op jit(solution)/shard_map/owner_update/pallas_call | solution.py:474
  153.7 4.7 %all-to-all-start = ((bf16[32,16,256]{2,1,0:T(8,128)(2,1)}), bf16[32,16,256]{2,1,0:T(8,128)(2,1)S(1)}, u32[]{:S(2)}, u32[]{:S(2)}) async-start(bf16[32,16,256]{2,1,0:T(8,128)(2,1)} %get-tuple-element.51), calls=%async_computation | async-start | bytes 524288 | tf_op jit(solution)/shard_map/all_to_all | solution.py:869
  158.4 0.0 copy-done.12
  158.4 0.0 copy-done.16
  158.4 0.0 copy-start.1
  158.4 0.0 copy-start.2
  158.4 0.0 copy-start.3
  158.5 0.0 copy-start.5
  158.5 0.0 copy-start.6
  158.5 0.0 copy-start.7
  158.5 0.0 copy-start.8
  158.5 28.6 %owner_basis.1 = (f32[1,512,512]{2,1,0:T(8,128)}, f32[1,256,256]{2,1,0:T(8,128)}, f32[1,512,512]{2,1,0:T(8,128)}, f32[1,256,256]{2,1,0:T(8,128)}) custom-call(s32[32]{0:T(128)S(1)} %copy-done.10, bf16[512,256]{1,0:T(8,128)(2,1)S(1)} %bitcast.23, f32[1,512,512]{2,1,0:T(8,128)S(1)} %copy-done.11, f32[1,256,256]{2,1,0:T(8,128)S(1)} %copy-done.15, ...), custom_call_target="tpu_custom_call" | custom-call | flops 30000001024 | bytes 4194304 | tf_op jit(solution)/shard_map/owner_basis/pallas_call | solution.py:474
  187.1 0.0 all-to-all-done.upd_ref
  187.1 0.0 copy-done.1
  187.1 0.0 copy-done.2
  187.1 0.0 copy-done.3
  187.1 0.0 copy-done.5
  187.1 0.0 copy-done.6
  187.2 0.0 copy-done.7
  187.2 0.0 copy-done.8
  187.2 1.4 new_weights.1
Async XLA Ops:
  31.4 117.2 %copy-start.11 = (f32[1,512,512]{2,1,0:T(8,128)S(1)}, f32[1,512,512]{2,1,0:T(8,128)}, u32[]{:S(2)}) copy-start(f32[1,512,512]{2,1,0:T(8,128)} %refs_0_.3) | copy-start | bytes 3145732
  31.4 117.2 %copy-start.13 = (f32[1,512,256]{2,1,0:T(8,128)S(1)}, f32[1,512,256]{2,1,0:T(8,128)}, u32[]{:S(2)}) copy-start(f32[1,512,256]{2,1,0:T(8,128)} %refs_0_.2) | copy-start | bytes 1572868
  31.5 117.2 %copy-start.14 = (f32[1,512,256]{2,1,0:T(8,128)S(1)}, f32[1,512,256]{2,1,0:T(8,128)}, u32[]{:S(2)}) copy-start(f32[1,512,256]{2,1,0:T(8,128)} %refs_1_.2) | copy-start | bytes 1572868
  31.5 117.2 %copy-start.15 = (f32[1,256,256]{2,1,0:T(8,128)S(1)}, f32[1,256,256]{2,1,0:T(8,128)}, u32[]{:S(2)}) copy-start(f32[1,256,256]{2,1,0:T(8,128)} %refs_1_.3) | copy-start | bytes 786436
  110.6 38.1 %copy-start.10 = (s32[32]{0:T(128)S(1)}, s32[32]{0:T(128)}, u32[]{:S(2)}) copy-start(s32[32]{0:T(128)} %get-tuple-element.47.inv_ref) | copy-start | bytes 388
  110.6 1.9 %copy-start = (bf16[24,256,256]{2,1,0:T(8,128)(2,1)S(1)}, bf16[24,256,256]{2,1,0:T(8,128)(2,1)}, u32[]{:S(2)}) copy-start(bf16[24,256,256]{2,1,0:T(8,128)(2,1)} %get-tuple-element.48.g_ref) | copy-start | bytes 9437188
  112.5 0.7 copy-start.4
  113.2 0.7 copy-start.9
  148.7 9.7 %copy-start.12 = (f32[1,512,512]{2,1,0:T(8,128)S(1)}, f32[1,512,512]{2,1,0:T(8,128)}, u32[]{:S(2)}) copy-start(f32[1,512,512]{2,1,0:T(8,128)} %refs_2_.3) | copy-start | bytes 3145732
  148.7 9.7 %copy-start.16 = (f32[1,256,256]{2,1,0:T(8,128)S(1)}, f32[1,256,256]{2,1,0:T(8,128)}, u32[]{:S(2)}) copy-start(f32[1,256,256]{2,1,0:T(8,128)} %refs_3_.3) | copy-start | bytes 786436
  153.7 33.4 %all-to-all-start = ((bf16[32,16,256]{2,1,0:T(8,128)(2,1)}), bf16[32,16,256]{2,1,0:T(8,128)(2,1)S(1)}, u32[]{:S(2)}, u32[]{:S(2)}) async-start(bf16[32,16,256]{2,1,0:T(8,128)(2,1)} %get-tuple-element.51), calls=%async_computation | async-start | bytes 524288 | tf_op jit(solution)/shard_map/all_to_all | solution.py:869
  158.4 28.7 %copy-start.1 = (f32[2,9,8,256]{3,2,1,0:T(8,128)S(1)}, f32[2,9,8,256]{3,2,1,0:T(8,128)}, u32[]{:S(2)}) copy-start(f32[2,9,8,256]{3,2,1,0:T(8,128)} %param.19) | copy-start | bytes 442372
  158.4 28.7 %copy-start.2 = (f32[4,8,256]{2,1,0:T(8,128)S(1)}, f32[4,8,256]{2,1,0:T(8,128)}, u32[]{:S(2)}) copy-start(f32[4,8,256]{2,1,0:T(8,128)} %attn_ref.3) | copy-start | bytes 98308
  158.4 28.7 %copy-start.3 = (f32[16,256]{1,0:T(8,128)S(1)}, f32[16,256]{1,0:T(8,128)}, u32[]{:S(2)}) copy-start(f32[16,256]{1,0:T(8,128)} %dense_ref.3) | copy-start | bytes 49156
  158.5 28.7 %copy-start.5 = (f32[12,8]{0,1:T(8,128)S(1)}, f32[12,8]{0,1:T(8,128)}, u32[]{:S(2)}) copy-start(f32[12,8]{0,1:T(8,128)} %param.22) | copy-start | bytes 1156
  158.5 28.7 %copy-start.6 = (f32[12,8]{0,1:T(8,128)S(1)}, f32[12,8]{0,1:T(8,128)}, u32[]{:S(2)}) copy-start(f32[12,8]{0,1:T(8,128)} %param.23) | copy-start | bytes 1156
  158.5 28.7 %copy-start.7 = (f32[12,8]{0,1:T(8,128)S(1)}, f32[12,8]{0,1:T(8,128)}, u32[]{:S(2)}) copy-start(f32[12,8]{0,1:T(8,128)} %param.24) | copy-start | bytes 1156
  158.5 28.7 %copy-start.8 = (s32[23]{0:T(128)S(1)}, s32[23]{0:T(128)}, u32[]{:S(2)}) copy-start(s32[23]{0:T(128)} %owners_ref.3) | copy-start | bytes 280
